TPU v7x, 512 devices: a whole 4x8x8 slice. The times are simulated.
512 devices in a mesh: replica: 64 (over x, z_lo, y), fsdp: 8 (over z_hi, core).
Axes of the slice: x: 4, y: 8, z: 8 (z_hi: 4, z_lo: 2; z = z_hi * 2 + z_lo), core: 2. Of those that a mesh axis runs over, the one named last changes fastest.
Arguments:
- tokens: bfloat16 [64, 1024, 8192], P('replica', 'fsdp'), may hold values from -6 to 6
- norm_gain: bfloat16 [64, 8192], P('replica'), may hold values from 0.25 to 1.75
- key_weight: bfloat16 [64, 8192, 512], P('replica', 'fsdp'), may hold values from -0.0625 to 0.0625
- key_target: bfloat16 [64, 1024, 512], P('replica', 'fsdp'), may hold values from -6 to 6
- outer_base: float32 [64, 8192], P('fsdp'), may hold values from -6 to 6
- outer_momentum: float32 [64, 8192], P('fsdp'), may hold values from -4 to 4
- replica_params: bfloat16 [64, 64, 8192], P('replica', 'fsdp'), may hold values from -6 to 6
Outputs:
- key_grad: bfloat16 [64, 8192, 512], P('replica', 'fsdp')
- base_next: float32 [64, 8192], P('fsdp')
- momentum_next: float32 [64, 8192], P('fsdp')
- params_next: bfloat16 [64, 64, 8192], P('replica', 'fsdp')
All inputs are finite; a program needn't handle non-finite values.
Results may differ from a plain program's by a relative error of at most 0.015.
Values may be sent and summed in bfloat16 or wider, within the bound.
No kernel may reach another device: no remote copies, remote signals or barrier semaphores. Data moves between devices by JAX's collectives and lax.ppermute only.
A program may use at most 64 MiB of HBM per device.

v0:
```python
import math

import jax
import jax.numpy as jnp
from jax import lax
from jax.sharding import PartitionSpec as P


def shards(tokens, norm_gain, key_weight, key_target, outer_base, outer_momentum, replica_params):
    values = tokens[0].astype(jnp.float32)
    scaled = lax.rsqrt(jnp.mean(values * values, axis=-1, keepdims=True) + 1e-05)
    normed = (values * scaled * norm_gain[0].astype(jnp.float32)[None, :]).astype(jnp.bfloat16)
    feats = lax.all_to_all(normed, "fsdp", split_axis=1, concat_axis=0, tiled=True)
    weights = key_weight[0]
    tok_rows = normed.shape[0]
    keys = jnp.dot(
        normed,
        lax.all_gather(weights, "fsdp", axis=0, tiled=True),
        preferred_element_type=jnp.float32,
    )
    all_tokens = tok_rows * lax.axis_size("fsdp")
    key_cot = ((keys - key_target[0].astype(jnp.float32)) * (1.0 / math.sqrt(all_tokens))).astype(
        jnp.bfloat16
    )
    cot_all = lax.all_gather(key_cot, "fsdp", axis=0, tiled=True)
    grad = lax.dot_general(
        feats, cot_all, (((0,), (0,)), ((), ())), preferred_element_type=jnp.float32
    )
    key_grad = grad.astype(jnp.bfloat16)[None]
    slab_rows = outer_base.shape[0]
    width = outer_base.shape[1]
    delta = outer_base - replica_params[0].astype(jnp.float32)
    blocks = delta.reshape(-1, 128)
    block_count = blocks.shape[0]
    block_scale = (jnp.max(jnp.abs(blocks), axis=-1) + 1e-06).astype(jnp.bfloat16)
    quant = (blocks * (448.0 / block_scale.astype(jnp.float32)[:, None])).astype(jnp.bfloat16)
    replicas = lax.axis_size("replica")
    momentum_flat = outer_momentum.reshape(-1, 128)
    base_flat = outer_base.reshape(-1, 128)
    quant_piece = lax.all_gather(quant, "replica", axis=0, tiled=True)
    scale_piece = lax.all_gather(block_scale, "replica", axis=0, tiled=True)
    count = quant_piece.shape[0] // block_count
    restored = quant_piece.astype(jnp.float32).reshape(count, block_count, 128)
    restored = restored * (scale_piece.astype(jnp.float32).reshape(count, block_count, 1) / 448.0)
    summed = jnp.sum(restored, axis=0)
    mean_delta = summed / replicas
    momentum_next = 0.9 * momentum_flat + mean_delta
    base_next = base_flat - 0.7 * (mean_delta + 0.9 * momentum_next)
    base_next = base_next.reshape(slab_rows, width)
    momentum_next = momentum_next.reshape(slab_rows, width)
    params_next = (0.5 * replica_params[0].astype(jnp.float32) + 0.5 * base_next).astype(
        jnp.bfloat16
    )[None]
    return (key_grad, base_next, momentum_next, params_next)


def solution(mesh):
    return jax.shard_map(
        shards,
        mesh=mesh,
        in_specs=(
            P("replica", "fsdp", None),
            P("replica", None),
            P("replica", "fsdp", None),
            P("replica", "fsdp", None),
            P("fsdp", None),
            P("fsdp", None),
            P("replica", "fsdp", None),
        ),
        out_specs=(
            P("replica", "fsdp", None),
            P("fsdp", None),
            P("fsdp", None),
            P("replica", "fsdp", None),
        ),
        check_vma=False,
    )
```

profile of v0, /device:TPU:1, one launch (start us, length us, event | category | flops | bytes accessed | tf_op | source)
XLA Modules:
  0.0 507.1 jit_solution(15085836065905186539)
XLA Ops:
  7.2 0.0 copy-start.5
  7.2 0.0 all-gather.10.cloned.1.call-start
  7.2 0.7 all-gather.10.cloned.1.call-update
  7.9 0.0 all-gather.8.cloned.1.call-start
  8.0 1.0 convert_subtract_fusion
  9.0 0.1 abs_reduce_fusion
  9.2 0.8 multiply_convert_fusion.1
  10.0 0.0 all-gather.8.cloned.1.call-update
  10.0 3.2 copy.13
  13.2 0.0 copy-done.5
  13.2 0.1 convert_reduce_fusion
  13.4 1.1 fusion.3
  14.5 2.6 multiply_convert_fusion
  17.1 0.0 copy-start.4
  17.1 11.9 %all-to-all-start = ((bf16[128,8,1024]{0,2,1:T(8,128)(2,1)}), bf16[128,8,1024]{0,2,1:T(8,128)(2,1)}, u32[]{:S(2)}, u32[]{:S(2)}) async-start(bf16[128,8,1024]{0,2,1:T(8,128)(2,1)} %multiply_convert_fusion), calls=%async_computation | async-start | bytes 4194304 | tf_op jit(solution)/shard_map/all_to_all | solution.py:13
  29.0 0.0 all-gather.6.cloned.1.call-start
  29.1 132.8 %all-gather.1 = bf16[64,1,512]{2,1,0:T(2,128)(2,1)S(1)} all-gather(bf16[1,1,512]{2,1,0:T(2,128)(2,1)S(1)} %reshape.82), channel_id=1, replica_groups=mesh['replica'=64,'fsdp'=8] {'replica'}, dimensions={0}, use_global_device_ids=true | all-gather | bytes 66560 | tf_op jit(solution)/shard_map/all_gather | solution.py:41
  161.9 0.2 convert_multiply_fusion.1
  162.1 0.0 all-to-all-done
  162.1 3.9 copy.14
  166.0 0.0 all-gather.10.cloned.1.call-done
  166.0 0.0 copy-done.4
  166.0 7.5 %fusion.21 = bf16[128,512]{1,0:T(8,128)(2,1)} fusion(bf16[1,8192,512]{2,1,0:T(8,128)(2,1)} %all-gather.10.cloned.1.call-done, bf16[1,128,8192]{1,2,0:T(8,128)(2,1)S(1)} %copy.13, f32[8192]{0:T(1024)S(1)} %bitcast.52, f32[128]{0:T(128)S(1)} %add_rsqrt_fusion, bf16[1,128,512]{2,1,0:T(8,128)(2,1)S(1)} %copy-done.4), kind=kOutput, calls=%fused_computation.17 | convolution fusion | flops 1078198272 | bytes 10781184 | tf_op jit(solution)/shard_map/dot_general | solution.py:16
  173.5 0.0 all-gather.6.cloned.1.call-update
  173.5 251.6 %all-gather.8.cloned.1.call-done = bf16[32768,128]{1,0:T(8,128)(2,1)} async-done(((bf16[512,128]{1,0:T(8,128)(2,1)}), bf16[32768,128]{1,0:T(8,128)(2,1)}) %all-gather.8.cloned.1.call-update) | async-done | bytes 8388624 | tf_op jit(solution)/shard_map/all_gather | solution.py:40
  425.1 0.0 copy-start.1
  425.1 0.0 copy-start.2
  425.1 0.0 copy-start.3
  425.1 0.0 copy-start
  425.1 8.5 %fusion = f32[512,128]{1,0:T(8,128)S(1)} fusion(bf16[64,512,128]{2,1,0:T(8,128)(2,1)} %bitcast.49, f32[64,512]{1,0:T(8,128)S(1)} %bitcast.51), kind=kLoop, calls=%fused_computation.1 | loop fusion | flops 12517376 | bytes 8781824 | tf_op jit(solution)/shard_map/reduce_sum | solution.py:45
  433.6 0.1 div.42
  433.7 0.0 copy-done.1
  433.7 0.0 copy-done.2
  433.7 0.0 copy-done.3
  433.7 0.9 fusion.28
  434.6 62.5 %all-gather.6.cloned.1.call-done = bf16[1024,512]{1,0:T(8,128)(2,1)} async-done(((bf16[128,512]{1,0:T(8,128)(2,1)}), bf16[1024,512]{1,0:T(8,128)(2,1)}) %all-gather.6.cloned.1.call-update) | async-done | bytes 1048592 | tf_op jit(solution)/shard_map/all_gather | solution.py:25
  497.1 0.0 copy-done
  497.1 3.5 fusion.10
  (8 shorter events, 0.1 us)
Async XLA Ops:
  7.2 6.1 %copy-start.5 = (bf16[1,8192]{1,0:T(2,128)(2,1)S(1)}, bf16[1,8192]{1,0:T(2,128)(2,1)}, u32[]{:S(2)}) copy-start(bf16[1,8192]{1,0:T(2,128)(2,1)} %param.8) | copy-start | bytes 49156
  7.2 158.8 %all-gather.10.cloned.1.call-start = ((), (), s32[]{:S(2)}) async-start(), calls=%async_computation.3 | async-start | bytes 9437184 | tf_op jit(solution)/shard_map/all_gather | solution.py:18
  7.9 417.2 %all-gather.8.cloned.1.call-start = ((), (), s32[]{:S(2)}) async-start(), calls=%async_computation.2 | async-start | bytes 8519680 | tf_op jit(solution)/shard_map/all_gather | solution.py:40
  17.1 148.9 %copy-start.4 = (bf16[1,128,512]{2,1,0:T(8,128)(2,1)S(1)}, bf16[1,128,512]{2,1,0:T(8,128)(2,1)}, u32[]{:S(2)}) copy-start(bf16[1,128,512]{2,1,0:T(8,128)(2,1)} %param.10) | copy-start | bytes 393220
  17.1 145.0 %all-to-all-start = ((bf16[128,8,1024]{0,2,1:T(8,128)(2,1)}), bf16[128,8,1024]{0,2,1:T(8,128)(2,1)}, u32[]{:S(2)}, u32[]{:S(2)}) async-start(bf16[128,8,1024]{0,2,1:T(8,128)(2,1)} %multiply_convert_fusion), calls=%async_computation | async-start | bytes 4194304 | tf_op jit(solution)/shard_map/all_to_all | solution.py:13
  29.0 468.0 %all-gather.6.cloned.1.call-start = ((), (), s32[]{:S(2)}) async-start(), calls=%async_computation.1 | async-start | bytes 1179648 | tf_op jit(solution)/shard_map/all_gather | solution.py:25
  425.1 8.6 %copy-start.1 = (f32[8,8192]{1,0:T(8,128)S(1)}, f32[8,8192]{1,0:T(8,128)}, u32[]{:S(2)}) copy-start(f32[8,8192]{1,0:T(8,128)} %param.11) | copy-start | bytes 786436
  425.1 8.6 %copy-start.2 = (bf16[1,8,8192]{2,1,0:T(8,128)(2,1)S(1)}, bf16[1,8,8192]{2,1,0:T(8,128)(2,1)}, u32[]{:S(2)}) copy-start(bf16[1,8,8192]{2,1,0:T(8,128)(2,1)} %param.13) | copy-start | bytes 393220
  425.1 8.6 %copy-start.3 = (f32[8,8192]{1,0:T(8,128)S(1)}, f32[8,8192]{1,0:T(8,128)}, u32[]{:S(2)}) copy-start(f32[8,8192]{1,0:T(8,128)} %param.12) | copy-start | bytes 786436
  425.1 72.0 %copy-start = (bf16[8,128,1024]{2,1,0:T(8,128)(2,1)S(1)}, bf16[8,128,1024]{2,1,0:T(8,128)(2,1)}, u32[]{:S(2)}) copy-start(bf16[8,128,1024]{2,1,0:T(8,128)(2,1)} %copy.14) | copy-start | bytes 6291460
Sparse Core Ops, SparseCore 0:
  10.2 139.4 all-gather.9
  152.3 272.7 all-gather.7
  427.8 69.1 all-gather.5
where the time goes:
time: 508 us; the launch traced here: 507 us
  waiting for transfers between devices  315 us (62%)
  blocking collectives  133 us (26%)
  other arithmetic  15.4 us (3%)
  between operations  13.9 us (3%)
  starting transfers between devices  12 us (2%)
  matrix products  11 us (2%)
  local copies, waits for them, and re-layouts  7.29 us (1%)
    all_gather x1, waiting for transfers between devices, shards(): quant_piece = lax.all_gather(quant, 'replica', axis=0, tiled=True)  252 us
    all_gather x1, blocking collectives, shards(): scale_piece = lax.all_gather(block_scale, 'replica', axis=0, tiled=True)  133 us
    all_gather x1, waiting for transfers between devices, shards(): cot_all = lax.all_gather(key_cot, 'fsdp', axis=0, tiled=True)  62.5 us
    all_to_all x1, starting transfers between devices, shards(): lax.all_to_all(normed, 'fsdp', split_axis=1, concat_axis=0, tiled=True)  11.9 us
  transfers between devices with their start and end apart: 4, of which 2 were waited for; matrix products, arithmetic and copies ran while one was open for 6% of the time, Pallas kernels for 0%

commit v1 on v0

v1 whole, which is shorter than its diff:
```python
import math

import jax
import jax.numpy as jnp
from jax import lax
from jax.sharding import PartitionSpec as P

XMODE = "a"
OUTER = "ag4"
BAR = 1
BACK = "a"
SPREAD = "g"
CHIPS = 4
CORES = 2
SAME = [[CORES * z + c for z in range(CHIPS)] for c in range(CORES)]
SWAP = [(i, i ^ 1) for i in range(CHIPS * CORES)]
ORDER = (2, 1, 3)
F32 = jnp.float32
BF16 = jnp.bfloat16


def mesh_groups(replicas):
    plane = [[r for r in range(replicas) if (r // 8) % 2 == z] for z in range(2)]
    pairs = [(r, r ^ 8) for r in range(replicas)]
    return plane, pairs


def hop(x, dz):
    pairs = [
        (CORES * z + c, CORES * ((z + dz) % CHIPS) + c) for z in range(CHIPS) for c in range(CORES)
    ]
    return lax.ppermute(x, "fsdp", pairs)


def chips_all_to_all(x):
    return lax.all_to_all(
        x, "fsdp", split_axis=0, concat_axis=0, axis_index_groups=SAME, tiled=True
    )


def stage_groups(replicas):
    parts = [[], [], []]
    for r in range(replicas):
        x, z, y = r // 16, (r // 8) % 2, r % 8
        keys = ((z, y), (x, z, y // 4), (x, y % 4))
        for part, key in zip(parts, keys):
            part.append((key, r))
    out = []
    for part in parts:
        names = sorted({key for key, _ in part})
        out.append([[r for key, r in part if key == name] for name in names])
    return out


def reduce_by_fours(x):
    for groups in stage_groups(lax.axis_size("replica")):
        got = lax.all_gather(x, "replica", axis=0, axis_index_groups=groups)
        total = jnp.sum(got.astype(F32), axis=0)
        x = total.astype(BF16)
    return total


def outer(outer_base, outer_momentum, params):
    rows, width = outer_base.shape
    replicas = lax.axis_size("replica")
    plane, pairs = mesh_groups(replicas)
    delta = outer_base - params.astype(F32)
    blocks = delta.reshape(rows, width // 128, 128)
    scale = (jnp.max(jnp.abs(blocks), axis=-1, keepdims=True) + 1e-06).astype(BF16).astype(F32)
    quant = (blocks * (448.0 / scale)).astype(BF16)
    restored = (quant.astype(F32) * (scale / 448.0)).astype(BF16)
    if OUTER == "ag4":
        total = reduce_by_fours(restored.reshape(-1, 128)).reshape(rows, width)
        return finish(outer_base, outer_momentum, params, total / replicas)
    members = len(plane[0])
    pieces = restored.reshape(members, rows * width // 128 // members, 128)
    got = lax.all_to_all(
        pieces, "replica", split_axis=0, concat_axis=0, axis_index_groups=plane, tiled=True
    )
    part = jnp.sum(got.astype(F32), axis=0)
    total = part + lax.ppermute(part, "replica", pairs)
    mean = (total / replicas).astype(BF16)
    spread = jnp.broadcast_to(mean[None], pieces.shape)
    mean_delta = lax.all_to_all(
        spread, "replica", split_axis=0, concat_axis=0, axis_index_groups=plane, tiled=True
    )
    return finish(outer_base, outer_momentum, params, mean_delta.reshape(rows, width).astype(F32))


def finish(outer_base, outer_momentum, params, mean_delta):
    momentum_next = 0.9 * outer_momentum + mean_delta
    base_next = outer_base - 0.7 * (mean_delta + 0.9 * momentum_next)
    params_next = (0.5 * params.astype(F32) + 0.5 * base_next).astype(BF16)
    return base_next, momentum_next, params_next


def shards(tokens, norm_gain, key_weight, key_target, outer_base, outer_momentum, replica_params):
    tok = tokens[0]
    rows, width = tok.shape
    weights = key_weight[0]
    depth, cols = weights.shape
    me = lax.axis_index("fsdp")
    core = me % CORES
    chip = me // CORES
    wide = CORES * depth
    root = 1.0 / math.sqrt(rows * CHIPS * CORES)
    dims = (((0,), (0,)), ((), ()))

    if XMODE == "a":
        x = chips_all_to_all(tok.reshape(rows, CHIPS, wide).transpose(1, 0, 2))
    else:
        got = {}
        for dz in (0,) + ORDER:
            piece = lax.dynamic_slice(tok, (0, (chip + dz) % CHIPS * wide), (rows, wide))
            got[dz] = hop(piece, dz) if dz else piece
        x = jnp.stack([got[dz] for dz in range(CHIPS)], axis=0)

    gain = lax.dynamic_slice(norm_gain[0], (me * depth,), (depth,)).astype(F32)[:, None]
    mine = (weights.astype(F32) * gain).astype(BF16)
    other = lax.ppermute(mine, "fsdp", SWAP)
    chip_weights = jnp.where(
        core == 0, jnp.concatenate([mine, other], 0), jnp.concatenate([other, mine], 0)
    )
    values = tok.astype(F32)
    inv = lax.rsqrt(jnp.mean(values * values, axis=-1, keepdims=True) + 1e-05)

    if BAR == 3:
        x, outer_base = lax.optimization_barrier((x, outer_base))
    base_next, momentum_next, params_next = outer(outer_base, outer_momentum, replica_params[0])
    if BAR == 1:
        x, base_next, momentum_next, params_next = lax.optimization_barrier((x, base_next, momentum_next, params_next))

    x = x.reshape(CHIPS * rows, wide)
    x_mine = lax.dynamic_slice(x, (0, core * depth), (CHIPS * rows, depth))
    x_send = lax.dynamic_slice(x, (0, (1 - core) * depth), (CHIPS * rows, depth))
    x_other = lax.ppermute(x_send, "fsdp", SWAP)
    part = jnp.dot(x, chip_weights, preferred_element_type=F32).astype(BF16).reshape(CHIPS, rows, cols)
    if XMODE == "p":
        order = (chip - jnp.arange(CHIPS)) % CHIPS
        part = jnp.take(part, order, axis=0)
    keys = jnp.sum(chips_all_to_all(part).astype(F32), axis=0)
    target = key_target[0].astype(F32)
    cot = ((keys * inv - target) * root * inv).astype(BF16)
    if SPREAD == "a":
        cots = chips_all_to_all(jnp.broadcast_to(cot[None], (CHIPS, rows, cols)))
    else:
        cots = lax.all_gather(cot, "fsdp", axis=0, axis_index_groups=SAME)
    if XMODE == "p":
        cots = jnp.take(cots, order, axis=0)
    cots = cots.reshape(CHIPS * rows, cols)
    cots_other = lax.ppermute(cots, "fsdp", SWAP)
    one = lax.dot_general(x_mine, cots, dims, preferred_element_type=F32)
    two = lax.dot_general(x_other, cots_other, dims, preferred_element_type=F32)
    key_grad = ((one + two) * gain).astype(BF16)[None]
    return (key_grad, base_next, momentum_next, params_next[None])


def solution(mesh):
    return jax.shard_map(
        shards,
        mesh=mesh,
        in_specs=(
            P("replica", "fsdp", None),
            P("replica", None),
            P("replica", "fsdp", None),
            P("replica", "fsdp", None),
            P("fsdp", None),
            P("fsdp", None),
            P("replica", "fsdp", None),
        ),
        out_specs=(
            P("replica", "fsdp", None),
            P("fsdp", None),
            P("fsdp", None),
            P("replica", "fsdp", None),
        ),
        check_vma=False,
    )
```

time: 508 us -> 127 us (0.25)
  the two profiles are of different devices: /device:TPU:1 before, /device:TPU:11 now
where the time goes in v1:
time: 127 us; the launch traced here: 126 us
  blocking collectives  62.9 us (50%)
  starting transfers between devices  38.8 us (31%)
  local copies, waits for them, and re-layouts  9.26 us (7%)
  matrix products  8.73 us (7%)
  other arithmetic  4.16 us (3%)
  waiting for transfers between devices  1.81 us (1%)
    all_gather x3, blocking collectives, reduce_by_fours(): got = lax.all_gather(x, 'replica', axis=0, axis_index_groups=groups)  47.9 us
    all_to_all x2, starting transfers between devices, chips_all_to_all(): lax.all_to_all(x, 'fsdp', split_axis=0, concat_axis=0, axis_index_groups=...  18.1 us
    all_gather x1, blocking collectives, shards(): cots = lax.all_gather(cot, 'fsdp', axis=0, axis_index_groups=SAME)  15.1 us
    ppermute x1, starting transfers between devices, shards(): cots_other = lax.ppermute(cots, 'fsdp', SWAP)  10.7 us
    ppermute x1, starting transfers between devices, shards(): x_other = lax.ppermute(x_send, 'fsdp', SWAP)  7.15 us
    unnamed x17, local copies, waits for them, and re-layouts  5.19 us
    dot_general x1, matrix products, shards(): jnp.dot(x, chip_weights, preferred_element_type=F32).astype(BF16)  5.03 us
    dot_general x1, matrix products, shards(): two = lax.dot_general(x_other, cots_other, dims, preferred_element_type=F32)  2.97 us
  transfers between devices with their start and end apart: 5, of which 2 were waited for; matrix products, arithmetic and copies ran while one was open for 7% of the time, Pallas kernels for 0%

profile of v1, /device:TPU:11, one launch (start us, length us, event | category | flops | bytes accessed | tf_op | source)
XLA Modules:
  0.0 126.5 jit_solution(13456290914902643527)
XLA Ops:
  0.6 4.1 %copy.23 = bf16[1,128,8192]{1,2,0:T(8,128)(2,1)} copy(bf16[1,128,8192]{2,1,0:T(8,128)(2,1)} %param.7) | data formatting | bytes 4194304 | tf_op args[0]
  4.7 0.0 copy-start.3
  4.7 10.1 %all-to-all-start = ((bf16[4,128,2048]{1,2,0:T(8,128)(2,1)}), bf16[4,128,2048]{1,2,0:T(8,128)(2,1)S(1)}, u32[]{:S(2)}, u32[]{:S(2)}) async-start(bf16[4,128,2048]{1,2,0:T(8,128)(2,1)} %bitcast.35), calls=%async_computation | async-start | bytes 4194304 | tf_op jit(solution)/shard_map/all_to_all | solution.py:36
  14.9 0.0 copy-start.4
  14.9 0.0 copy-start.5
  14.9 0.7 dynamic-slice_convert_fusion
  15.6 0.0 copy-done.3
  15.6 1.3 fusion.6
  16.9 2.9 %collective-permute-start = (bf16[1024,512]{1,0:T(8,128)(2,1)}, bf16[1024,512]{1,0:T(8,128)(2,1)}, u32[]{:S(2)}, u32[]{:S(2)}) collective-permute-start(bf16[1024,512]{1,0:T(8,128)(2,1)} %fusion.6), channel_id=1, source_target_pairs={{0,1},{1,0},{2,3},{3,2},{4,5},{5,4},{6,7},{7,6},{8,9},{9,8},{10,11... | collective-permute-start | bytes 3145736 | tf_op jit(solution)/shard_map/ppermute | solution.py:120
  19.8 0.0 copy-done.4
  19.8 0.0 copy-done.5
  19.8 0.1 bitcast_reduce_fusion
  19.9 0.1 copy.24
  20.0 0.1 div.31
  20.1 0.1 div.33
  20.1 0.1 reshape.150
  20.2 0.2 multiply_convert_fusion.1
  20.4 11.1 %all_gather.19 = bf16[4,512,128]{2,1,0:T(8,128)(2,1)S(1)} all-gather(bf16[1,512,128]{2,1,0:T(8,128)(2,1)S(1)} %multiply_convert_fusion.1), channel_id=1, replica_groups={{0,128,256,384},{8,136,264,392},{16,144,272,400},{24,152,280,408},{32,1..., dimensions={0}, use_global_device_ids=true | all-gather | bytes 655360 | tf_op jit(solution)/shard_map/all_gather | solution.py:57
  31.6 0.0 copy-start.6
  31.6 0.1 reduce_sum.53
  31.6 12.9 %all-gather = bf16[2048,128]{1,0:T(8,128)(2,1)S(1)} all-gather(bf16[512,128]{1,0:T(8,128)(2,1)S(1)} %reduce_sum.53), channel_id=2, replica_groups={{0,8,16,24},{32,40,48,56},{64,72,80,88},{96,104,112,120},{128,136,144,1..., dimensions={0}, use_global_device_ids=true | all-gather | bytes 655360 | tf_op jit(solution)/shard_map/all_gather | solution.py:57
  44.5 0.1 reduce_sum.54
  44.6 23.8 %all-gather.1 = bf16[2048,128]{1,0:T(8,128)(2,1)S(1)} all-gather(bf16[512,128]{1,0:T(8,128)(2,1)S(1)} %reduce_sum.54), channel_id=3, replica_groups={{0,32,64,96},{8,40,72,104},{16,48,80,112},{24,56,88,120},{128,160,192,2..., dimensions={0}, use_global_device_ids=true | all-gather | bytes 655360 | tf_op jit(solution)/shard_map/all_gather | solution.py:57
  68.4 0.1 convert_reduce_fusion
  68.5 0.1 div.36
  68.6 0.0 copy-done.6
  68.6 0.9 fusion.13
  69.5 0.0 all-to-all-done
  69.5 2.7 %copy.25 = bf16[4,128,2048]{2,1,0:T(8,128)(2,1)} copy(bf16[4,128,2048]{1,2,0:T(8,128)(2,1)S(1)} %all-to-all-done) | data formatting | bytes 4194304 | tf_op jit(solution)/shard_map/optimization_barrier | solution.py:131
  72.2 0.0 collective-permute-done
  72.2 5.0 %fusion.9 = bf16[512,512]{1,0:T(8,128)(2,1)} fusion(bf16[512,2048]{1,0:T(8,128)(2,1)} %bitcast.36, bf16[1024,512]{1,0:T(8,128)(2,1)} %collective-permute-done, bf16[1024,512]{1,0:T(8,128)(2,1)} %fusion.6, pred[]{:T(512)S(6)} %eq.5), kind=kOutput, calls=%fused_computation.13 | convolution fusion | flops 1083441152 | bytes 4718593 | tf_op jit(solution)/shard_map/dot_general | solution.py:137
  77.2 7.9 %all-to-all-start.1 = ((bf16[4,128,512]{2,1,0:T(8,128)(2,1)}), bf16[4,128,512]{2,1,0:T(8,128)(2,1)S(1)}, u32[]{:S(2)}, u32[]{:S(2)}) async-start(bf16[4,128,512]{2,1,0:T(8,128)(2,1)} %bitcast.10), calls=%async_computation.1 | async-start | bytes 1048576 | tf_op jit(solution)/shard_map/all_to_all | solution.py:36
  85.2 0.0 copy-done
  85.2 0.5 multiply_reduce_fusion
  85.7 1.1 copy-done.1
  86.8 1.1 constant_dynamic-slice_fusion
  87.8 7.1 %collective-permute-start.1 = (bf16[512,1024]{1,0:T(8,128)(2,1)}, bf16[512,1024]{1,0:T(8,128)(2,1)}, u32[]{:S(2)}, u32[]{:S(2)}) collective-permute-start(bf16[512,1024]{1,0:T(8,128)(2,1)} %constant_dynamic-slice_fusion), channel_id=1, source_target_pairs={{0,1},{1,0},{2,3},{3,2},{4,5},{5,4},{6,7},{7,6},{8,9},{9,8},{10,11... | collective-permute-start | bytes 3145736 | tf_op jit(solution)/shard_map/ppermute | solution.py:136
  95.0 1.1 all-to-all-done.1
  96.0 0.1 convert_reduce_fusion.1
  96.1 0.0 copy-done.7
  96.1 0.1 fusion.16
  96.2 15.1 %all_gather.24 = bf16[4,128,512]{2,1,0:T(8,128)(2,1)S(1)} all-gather(bf16[1,128,512]{2,1,0:T(8,128)(2,1)S(1)} %fusion.16), channel_id=1, replica_groups={{0,2,4,6},{1,3,5,7},{8,10,12,14},{9,11,13,15},{16,18,20,22},{17,19,21,2..., dimensions={0}, use_global_device_ids=true | all-gather | bytes 655360 | tf_op jit(solution)/shard_map/all_gather | solution.py:147
  111.3 10.7 %collective-permute-start.2 = (bf16[512,512]{1,0:T(8,128)(2,1)S(1)}, bf16[512,512]{1,0:T(8,128)(2,1)S(1)}, u32[]{:S(2)}, u32[]{:S(2)}) collective-permute-start(bf16[512,512]{1,0:T(8,128)(2,1)S(1)} %bitcast.41), channel_id=1, source_target_pairs={{0,1},{1,0},{2,3},{3,2},{4,5},{5,4},{6,7},{7,6},{8,9},{9,8},{10,11... | collective-permute-start | bytes 1572872 | tf_op jit(solution)/shard_map/ppermute | solution.py:151
  122.0 0.0 copy-done.2
  122.0 0.7 fusion.10
  122.8 0.0 collective-permute-done.1
  122.8 0.7 collective-permute-done.2
  123.5 3.0 %fusion.8 = bf16[1,1024,512]{2,1,0:T(8,128)(2,1)} fusion(f32[1024,512]{1,0:T(8,128)S(1)} %fusion.10, bf16[512,1024]{1,0:T(8,128)(2,1)} %collective-permute-done.1, bf16[512,512]{1,0:T(8,128)(2,1)S(1)} %collective-permute-done.2, f32[1024]{0:T(1024)S(1)} %bitcast.45), kind=kOutput, calls=%fused_computation.12 | convolution fusion | flops 538443776 | bytes 4722688 | tf_op jit(solution)/shard_map/dot_general | solution.py:153
  (7 shorter events, 0.0 us)
Async XLA Ops:
  4.7 10.9 %copy-start.3 = (bf16[1,1024,512]{2,1,0:T(8,128)(2,1)S(1)}, bf16[1,1024,512]{2,1,0:T(8,128)(2,1)}, u32[]{:S(2)}) copy-start(bf16[1,1024,512]{2,1,0:T(8,128)(2,1)} %param.9) | copy-start | bytes 3145732
  4.7 64.8 %all-to-all-start = ((bf16[4,128,2048]{1,2,0:T(8,128)(2,1)}), bf16[4,128,2048]{1,2,0:T(8,128)(2,1)S(1)}, u32[]{:S(2)}, u32[]{:S(2)}) async-start(bf16[4,128,2048]{1,2,0:T(8,128)(2,1)} %bitcast.35), calls=%async_computation | async-start | bytes 4194304 | tf_op jit(solution)/shard_map/all_to_all | solution.py:36
  14.9 4.9 %copy-start.4 = (f32[8,8192]{1,0:T(8,128)S(1)}, f32[8,8192]{1,0:T(8,128)}, u32[]{:S(2)}) copy-start(f32[8,8192]{1,0:T(8,128)} %param.11) | copy-start | bytes 786436
  14.9 4.9 %copy-start.5 = (bf16[1,8,8192]{2,1,0:T(8,128)(2,1)S(1)}, bf16[1,8,8192]{2,1,0:T(8,128)(2,1)}, u32[]{:S(2)}) copy-start(bf16[1,8,8192]{2,1,0:T(8,128)(2,1)} %param.13) | copy-start | bytes 393220
  16.9 55.3 %collective-permute-start = (bf16[1024,512]{1,0:T(8,128)(2,1)}, bf16[1024,512]{1,0:T(8,128)(2,1)}, u32[]{:S(2)}, u32[]{:S(2)}) collective-permute-start(bf16[1024,512]{1,0:T(8,128)(2,1)} %fusion.6), channel_id=1, source_target_pairs={{0,1},{1,0},{2,3},{3,2},{4,5},{5,4},{6,7},{7,6},{8,9},{9,8},{10,11... | collective-permute-start | bytes 3145736 | tf_op jit(solution)/shard_map/ppermute | solution.py:120
  31.6 37.0 %copy-start.6 = (f32[8,8192]{1,0:T(8,128)S(1)}, f32[8,8192]{1,0:T(8,128)}, u32[]{:S(2)}) copy-start(f32[8,8192]{1,0:T(8,128)} %param.12) | copy-start | bytes 786436
  72.2 13.0 %copy-start = (bf16[1,128,8192]{2,1,0:T(8,128)(2,1)S(1)}, bf16[1,128,8192]{2,1,0:T(8,128)(2,1)}, u32[]{:S(2)}) copy-start(bf16[1,128,8192]{2,1,0:T(8,128)(2,1)} %param.7) | copy-start | bytes 6291460
  77.2 18.8 %all-to-all-start.1 = ((bf16[4,128,512]{2,1,0:T(8,128)(2,1)}), bf16[4,128,512]{2,1,0:T(8,128)(2,1)S(1)}, u32[]{:S(2)}, u32[]{:S(2)}) async-start(bf16[4,128,512]{2,1,0:T(8,128)(2,1)} %bitcast.10), calls=%async_computation.1 | async-start | bytes 1048576 | tf_op jit(solution)/shard_map/all_to_all | solution.py:36
  85.2 1.6 %copy-start.1 = (bf16[4,128,2048]{2,1,0:T(8,128)(2,1)S(1)}, bf16[4,128,2048]{2,1,0:T(8,128)(2,1)}, u32[]{:S(2)}) copy-start(bf16[4,128,2048]{2,1,0:T(8,128)(2,1)} %copy.25) | copy-start | bytes 6291460
  85.2 10.9 %copy-start.7 = (bf16[1,128,512]{2,1,0:T(8,128)(2,1)S(1)}, bf16[1,128,512]{2,1,0:T(8,128)(2,1)}, u32[]{:S(2)}) copy-start(bf16[1,128,512]{2,1,0:T(8,128)(2,1)} %param.10) | copy-start | bytes 393220
  85.7 36.3 %copy-start.2 = (bf16[4,128,2048]{2,1,0:T(8,128)(2,1)S(1)}, bf16[4,128,2048]{2,1,0:T(8,128)(2,1)}, u32[]{:S(2)}) copy-start(bf16[4,128,2048]{2,1,0:T(8,128)(2,1)} %copy.25) | copy-start | bytes 6291460
  87.8 34.9 %collective-permute-start.1 = (bf16[512,1024]{1,0:T(8,128)(2,1)}, bf16[512,1024]{1,0:T(8,128)(2,1)}, u32[]{:S(2)}, u32[]{:S(2)}) collective-permute-start(bf16[512,1024]{1,0:T(8,128)(2,1)} %constant_dynamic-slice_fusion), channel_id=1, source_target_pairs={{0,1},{1,0},{2,3},{3,2},{4,5},{5,4},{6,7},{7,6},{8,9},{9,8},{10,11... | collective-permute-start | bytes 3145736 | tf_op jit(solution)/shard_map/ppermute | solution.py:136
  111.3 12.2 %collective-permute-start.2 = (bf16[512,512]{1,0:T(8,128)(2,1)S(1)}, bf16[512,512]{1,0:T(8,128)(2,1)S(1)}, u32[]{:S(2)}, u32[]{:S(2)}) collective-permute-start(bf16[512,512]{1,0:T(8,128)(2,1)S(1)} %bitcast.41), channel_id=1, source_target_pairs={{0,1},{1,0},{2,3},{3,2},{4,5},{5,4},{6,7},{7,6},{8,9},{9,8},{10,11... | collective-permute-start | bytes 1572872 | tf_op jit(solution)/shard_map/ppermute | solution.py:151

commit v2 on v0

v2 whole, which is shorter than its diff:
```python
import math

import jax
import jax.numpy as jnp
from jax import lax
from jax.experimental import pallas as pl
from jax.experimental.pallas import tpu as pltpu
from jax.sharding import PartitionSpec as P

CHIPS = 4
CORES = 2
SAME = [[CORES * z + c for z in range(CHIPS)] for c in range(CORES)]
SWAP = [(i, i ^ 1) for i in range(CHIPS * CORES)]
F32 = jnp.float32
BF16 = jnp.bfloat16
LIMIT = 40 << 20


def chips_all_to_all(x):
    return lax.all_to_all(
        x, "fsdp", split_axis=0, concat_axis=0, axis_index_groups=SAME, tiled=True
    )


def split_kernel(tok, out, held, come, go):
    wide = out.shape[2]
    ins = [
        pltpu.make_async_copy(tok.at[:, pl.ds(z * wide, wide)], held.at[z], come.at[z])
        for z in range(CHIPS)
    ]
    outs = [pltpu.make_async_copy(held.at[z], out.at[z], go.at[z]) for z in range(CHIPS)]
    for copy in ins:
        copy.start()
    for copy, after in zip(ins, outs):
        copy.wait()
        after.start()
    for after in outs:
        after.wait()


def split_features(tok):
    rows, width = tok.shape
    shape = (CHIPS, rows, width // CHIPS)
    return pl.pallas_call(
        split_kernel,
        out_shape=jax.ShapeDtypeStruct(shape, tok.dtype),
        in_specs=[pl.BlockSpec(memory_space=pl.ANY)],
        out_specs=pl.BlockSpec(memory_space=pl.ANY),
        scratch_shapes=[
            pltpu.VMEM(shape, tok.dtype),
            pltpu.SemaphoreType.DMA((CHIPS,)),
            pltpu.SemaphoreType.DMA((CHIPS,)),
        ],
        cost_estimate=pl.CostEstimate(flops=0, bytes_accessed=4 * rows * width, transcendentals=0),
    )(tok)


def keys_kernel(core, x, mine, other, out):
    chips, rows, wide = x.shape
    depth, cols = mine.shape
    near = x[:, :, pl.ds(pl.multiple_of(core[0] * depth, depth), depth)]
    far = x[:, :, pl.ds(pl.multiple_of((1 - core[0]) * depth, depth), depth)]
    near = near.reshape(chips * rows, depth)
    far = far.reshape(chips * rows, depth)
    for at in range(0, cols, 256):
        part = pl.ds(at, 256)
        total = jnp.dot(near, mine[:, part], preferred_element_type=F32)
        total = total + jnp.dot(far, other[:, part], preferred_element_type=F32)
        out[:, :, part] = total.astype(out.dtype).reshape(chips, rows, 256)


def partial_keys(core, x, mine, other):
    chips, rows, wide = x.shape
    cols = mine.shape[1]
    vmem = pl.BlockSpec(memory_space=pltpu.VMEM)
    return pl.pallas_call(
        keys_kernel,
        in_specs=[pl.BlockSpec(memory_space=pltpu.SMEM), vmem, vmem, vmem],
        out_specs=vmem,
        out_shape=jax.ShapeDtypeStruct((chips, rows, cols), BF16),
        compiler_params=pltpu.CompilerParams(vmem_limit_bytes=24 << 20),
        cost_estimate=pl.CostEstimate(
            flops=2 * chips * rows * wide * cols,
            bytes_accessed=2 * (chips * rows * (wide + cols) + wide * cols),
            transcendentals=0,
        ),
    )(core, x, mine, other)


def quantize_kernel(base, params, out):
    for k in range(base.shape[1] // 128):
        at = pl.ds(k * 128, 128)
        delta = base[:, at] - params[:, at].astype(F32)
        scale = (jnp.max(jnp.abs(delta), axis=-1, keepdims=True) + 1e-06).astype(BF16).astype(F32)
        quant = (delta * (448.0 / scale)).astype(BF16)
        out[:, at] = (quant.astype(F32) * (scale / 448.0)).astype(BF16)


def quantize(base, params):
    return pl.pallas_call(
        quantize_kernel,
        out_shape=jax.ShapeDtypeStruct(base.shape, BF16),
        cost_estimate=pl.CostEstimate(
            flops=8 * base.size, bytes_accessed=8 * base.size, transcendentals=0
        ),
    )(base, params)


def fours_along_x(replicas):
    return [[r for r in range(replicas) if r % 16 == k] for k in range(16)]


def fours_along_y(replicas):
    return [[4 * b + j for j in range(4)] for b in range(replicas // 4)]


def sum_of_sixteen(x):
    replicas = lax.axis_size("replica")
    for groups in (fours_along_x(replicas), fours_along_y(replicas)):
        got = lax.all_gather(x.astype(BF16), "replica", axis=0, axis_index_groups=groups)
        x = jnp.sum(got.astype(F32), axis=0)
    return x


def add_neighbour(x, bit):
    pairs = [(r, r ^ bit) for r in range(lax.axis_size("replica"))]
    return x + lax.ppermute(x.astype(BF16), "replica", pairs).astype(F32)


def shards(tokens, norm_gain, key_weight, key_target, outer_base, outer_momentum, replica_params):
    tok = tokens[0]
    rows, width = tok.shape
    weights = key_weight[0]
    depth, cols = weights.shape
    me = lax.axis_index("fsdp")
    core = me % CORES
    this_core = core[None].astype(jnp.int32)
    wide = CORES * depth
    root = 1.0 / math.sqrt(rows * CHIPS * CORES)
    dims = (((0,), (0,)), ((), ()))

    x = chips_all_to_all(split_features(tok))

    gain = lax.dynamic_slice(norm_gain[0], (me * depth,), (depth,)).astype(F32)[:, None]
    mine = (weights.astype(F32) * gain).astype(BF16)
    other = lax.ppermute(mine, "fsdp", SWAP)
    values = tok.astype(F32)
    inv = lax.rsqrt(jnp.mean(values * values, axis=-1, keepdims=True) + 1e-05)

    slope = root * inv
    offset = key_target[0].astype(F32) * slope
    slope = slope * inv
    summed = sum_of_sixteen(add_neighbour(quantize(outer_base, replica_params[0]), 4))

    x, summed, slope, offset = lax.optimization_barrier((x, summed, slope, offset))

    part = partial_keys(this_core, x, mine, other)
    parts = chips_all_to_all(part)
    x = x.reshape(CHIPS * rows, wide)
    x_mine = lax.dynamic_slice(x, (0, core * depth), (CHIPS * rows, depth))
    x_send = lax.dynamic_slice(x, (0, (1 - core) * depth), (CHIPS * rows, depth))
    x_other = lax.ppermute(x_send, "fsdp", SWAP)

    mean_delta = add_neighbour(summed, 8) / lax.axis_size("replica")
    momentum_next = 0.9 * outer_momentum + mean_delta
    base_next = outer_base - 0.7 * (mean_delta + 0.9 * momentum_next)
    params_next = (0.5 * replica_params.astype(F32) + 0.5 * base_next[None]).astype(BF16)

    keys = jnp.sum(parts.astype(F32), axis=0)
    cot = (keys * slope - offset).astype(BF16)
    cots = lax.all_gather(cot, "fsdp", axis=0, axis_index_groups=SAME)
    cots = cots.reshape(CHIPS * rows, cols)
    cots_other = lax.ppermute(cots, "fsdp", SWAP)
    one = lax.dot_general(x_mine, cots, dims, preferred_element_type=F32)
    two = lax.dot_general(x_other, cots_other, dims, preferred_element_type=F32)
    key_grad = ((one + two) * gain).astype(BF16)[None]
    return (key_grad, base_next, momentum_next, params_next)


def solution(mesh):
    return jax.shard_map(
        shards,
        mesh=mesh,
        in_specs=(
            P("replica", "fsdp", None),
            P("replica", None),
            P("replica", "fsdp", None),
            P("replica", "fsdp", None),
            P("fsdp", None),
            P("fsdp", None),
            P("replica", "fsdp", None),
        ),
        out_specs=(
            P("replica", "fsdp", None),
            P("fsdp", None),
            P("fsdp", None),
            P("replica", "fsdp", None),
        ),
        check_vma=False,
    )
```

time: 508 us -> 110 us (0.22)
  waiting for transfers between devices: 315 us -> 0.02 us
  blocking collectives: 133 us -> 39.9 us
  starting transfers between devices: 12 us -> 48.8 us
  between operations: 13.9 us -> 0.88 us
  other arithmetic: 15.4 us -> 6.5 us
  matrix products: 11 us -> 3.71 us
  Pallas kernels: 0 us -> 6.76 us
  local copies, waits for them, and re-layouts: 7.29 us -> 1.89 us
    all_gather x3 -> x0, waiting for transfers between devices: 314 us -> none  [the longest x1 252 us: shards(): quant_piece = lax.all_gather(quant, 'replica', axis=0, tiled=True)]
    all_gather x1 -> x3, blocking collectives: 133 us -> 39.9 us  [the longest x2 23.9 us: sum_of_sixteen(): lax.all_gather(x.astype(BF16), 'replica', axis=0, axis_index_groups=groups)]
    ppermute x0 -> x5, starting transfers between devices: none -> 27 us  [the longest x2 11.2 us: add_neighbour(): return x + lax.ppermute(x.astype(BF16), 'replica', pairs).astype(F32)]
    all_to_all x1 -> x2, starting transfers between devices: 11.9 us -> 21.8 us  [chips_all_to_all(): lax.all_to_all(x, 'fsdp', split_axis=0, concat_axis=0, axis_index_groups=...]
    reduce_sum x2 -> x4, other arithmetic: 9.55 us -> 0.69 us  [the longest x1 0.49 us: shards(): inv = lax.rsqrt(jnp.mean(values * values, axis=-1, keepdims=True) + 1e-05)]
    dot_general x2, matrix products: 11 us -> 3.71 us  [the longest x1 2.97 us: shards(): two = lax.dot_general(x_other, cots_other, dims, preferred_element_type=F32)]
    pallas_call x0 -> x3, Pallas kernels: none -> 6.76 us  [the longest x1 2.47 us: split_features(): pl.pallas_call(split_kernel, out_shape=jax.ShapeDtypeStruct(shape, tok.dt...]
  transfers between devices with their start and end apart: 4 -> 7, of which waited for: 2 -> 0; matrix products, arithmetic and copies ran while one was open for 6% -> 8% of each run, Pallas kernels for 0% -> 2%
where the time goes in v2:
time: 110 us; the launch traced here: 109 us
  starting transfers between devices  48.8 us (44%)
  blocking collectives  39.9 us (36%)
  Pallas kernels  6.76 us (6%)
  other arithmetic  6.5 us (6%)
  matrix products  3.71 us (3%)
  local copies, waits for them, and re-layouts  1.89 us (2%)
    all_gather x2, blocking collectives, sum_of_sixteen(): lax.all_gather(x.astype(BF16), 'replica', axis=0, axis_index_groups=groups)  23.9 us
    all_to_all x2, starting transfers between devices, chips_all_to_all(): lax.all_to_all(x, 'fsdp', split_axis=0, concat_axis=0, axis_index_groups=...  21.8 us
    all_gather x1, blocking collectives, shards(): cots = lax.all_gather(cot, 'fsdp', axis=0, axis_index_groups=SAME)  16 us
    ppermute x2, starting transfers between devices, add_neighbour(): return x + lax.ppermute(x.astype(BF16), 'replica', pairs).astype(F32)  11.2 us
    ppermute x1, starting transfers between devices, shards(): cots_other = lax.ppermute(cots, 'fsdp', SWAP)  7.97 us
    ppermute x1, starting transfers between devices, shards(): x_other = lax.ppermute(x_send, 'fsdp', SWAP)  4.72 us
    ppermute x1, starting transfers between devices, shards(): other = lax.ppermute(mine, 'fsdp', SWAP)  3.14 us
    dot_general x1, matrix products, shards(): two = lax.dot_general(x_other, cots_other, dims, preferred_element_type=F32)  2.97 us
  transfers between devices with their start and end apart: 7, of which 0 were waited for; matrix products, arithmetic and copies ran while one was open for 8% of the time, Pallas kernels for 2%

profile of v2, /device:TPU:1, one launch (start us, length us, event | category | flops | bytes accessed | tf_op | source)
XLA Modules:
  0.0 108.5 jit_solution(7931636504400328148)
XLA Ops:
  0.6 2.5 %shard_map.102 = bf16[4,128,2048]{2,1,0:T(8,128)(2,1)} custom-call(bf16[128,8192]{1,0:T(8,128)(2,1)} %bitcast.33), custom_call_target="tpu_custom_call" | custom-call | bytes 4194304 | tf_op jit(solution)/shard_map/pallas_call | solution.py:44
  3.1 10.9 %all-to-all-start = ((bf16[4,128,2048]{2,1,0:T(8,128)(2,1)}), bf16[4,128,2048]{2,1,0:T(8,128)(2,1)S(1)}, u32[]{:S(2)}, u32[]{:S(2)}) async-start(bf16[4,128,2048]{2,1,0:T(8,128)(2,1)} %shard_map.102), calls=%async_computation | async-start | bytes 4194304 | tf_op jit(solution)/shard_map/all_to_all | solution.py:20
  14.0 1.8 %shard_map.103 = bf16[8,8192]{1,0:T(8,128)(2,1)} custom-call(f32[8,8192]{1,0:T(8,128)} %base.1, bf16[8,8192]{1,0:T(8,128)(2,1)} %bitcast.34), custom_call_target="tpu_custom_call" | custom-call | flops 524288 | bytes 524288 | tf_op jit(solution)/shard_map/pallas_call | solution.py:100
  15.8 7.4 %collective-permute-start = (bf16[8,8192]{1,0:T(8,128)(2,1)}, bf16[8,8192]{1,0:T(8,128)(2,1)S(1)}, u32[]{:S(2)}, u32[]{:S(2)}) collective-permute-start(bf16[8,8192]{1,0:T(8,128)(2,1)} %shard_map.103), channel_id=1, source_target_pairs={{0,32},{8,40},{16,48},{24,56},{32,0},{40,8},{48,16},{56,24},{64,96... | collective-permute-start | bytes 393224 | tf_op jit(solution)/shard_map/ppermute | solution.py:127
  23.2 0.0 copy-start.1
  23.3 0.8 dynamic-slice_convert_fusion
  24.1 0.0 copy-start.7
  24.1 0.0 copy-start.4
  24.1 1.6 %fusion.mine = bf16[1024,512]{1,0:T(8,128)(2,1)S(1)} fusion(bf16[1,1024,512]{2,1,0:T(8,128)(2,1)} %param.9, f32[1024]{0:T(1024)S(1)} %bitcast.35), kind=kLoop, calls=%fused_computation.2 | loop fusion | flops 1572864 | bytes 2101248 | tf_op jit(solution)/shard_map/convert_element_type | solution.py:145
  25.7 3.1 %collective-permute-start.1 = (bf16[1024,512]{1,0:T(8,128)(2,1)S(1)}, bf16[1024,512]{1,0:T(8,128)(2,1)}, u32[]{:S(2)}, u32[]{:S(2)}) collective-permute-start(bf16[1024,512]{1,0:T(8,128)(2,1)S(1)} %fusion.mine), channel_id=1, source_target_pairs={{0,1},{1,0},{2,3},{3,2},{4,5},{5,4},{6,7},{7,6},{8,9},{9,8},{10,11... | collective-permute-start | bytes 3145736 | tf_op jit(solution)/shard_map/ppermute | solution.py:146
  28.8 0.0 copy-done.1
  28.8 0.5 multiply_reduce_fusion
  29.3 0.0 copy-done.7
  29.3 0.8 convert_multiply_fusion.1
  30.1 0.0 collective-permute-done
  30.1 0.0 copy-done.4
  30.2 11.4 %all-gather = bf16[32,8192]{1,0:T(8,128)(2,1)S(1)} all-gather(bf16[8,8192]{1,0:T(8,128)(2,1)S(1)} %add_convert_fusion), channel_id=2, replica_groups={{0,128,256,384},{8,136,264,392},{16,144,272,400},{24,152,280,408},{32,1..., dimensions={0}, use_global_device_ids=true | all-gather | bytes 655360 | tf_op jit(solution)/shard_map/all_gather | solution.py:120
  41.6 0.1 bitcast_reduce_fusion
  41.7 12.5 %all-gather.1 = bf16[32,8192]{1,0:T(8,128)(2,1)S(1)} all-gather(bf16[8,8192]{1,0:T(8,128)(2,1)S(1)} %bitcast_reduce_fusion), channel_id=3, replica_groups={{0,8,16,24},{32,40,48,56},{64,72,80,88},{96,104,112,120},{128,136,144,1..., dimensions={0}, use_global_device_ids=true | all-gather | bytes 655360 | tf_op jit(solution)/shard_map/all_gather | solution.py:120
  54.2 0.1 convert_reduce_fusion
  54.3 0.0 all-to-all-done.x
  54.3 0.0 collective-permute-done.1.other
  54.3 2.5 %shard_map.104 = bf16[4,128,512]{2,1,0:T(8,128)(2,1)S(1)} custom-call(s32[1]{0:T(128)} %bitcast.7.core, bf16[4,128,2048]{2,1,0:T(8,128)(2,1)S(1)} %all-to-all-done.x, bf16[1024,512]{1,0:T(8,128)(2,1)S(1)} %fusion.mine, bf16[1024,512]{1,0:T(8,128)(2,1)} %collective-permute-done.1.other), custom_call_target="tpu_custom_call" | custom-call | flops 1073741824 | bytes 4718592 | tf_op jit(solution)/shard_map/pallas_call | solution.py:76
  56.7 0.0 copy-start
  56.8 0.8 copy-done
  57.6 0.0 copy-start.2
  57.6 11.0 %all-to-all-start.1 = ((bf16[4,128,512]{2,1,0:T(8,128)(2,1)}), bf16[4,128,512]{2,1,0:T(8,128)(2,1)S(1)}, u32[]{:S(2)}, u32[]{:S(2)}) async-start(bf16[4,128,512]{2,1,0:T(8,128)(2,1)} %copy-done), calls=%async_computation.1 | async-start | bytes 1048576 | tf_op jit(solution)/shard_map/all_to_all | solution.py:20
  68.5 0.0 copy-start.5
  68.5 1.1 constant_dynamic-slice_fusion
  69.6 4.7 %collective-permute-start.2 = (bf16[512,1024]{1,0:T(8,128)(2,1)}, bf16[512,1024]{1,0:T(8,128)(2,1)}, u32[]{:S(2)}, u32[]{:S(2)}) collective-permute-start(bf16[512,1024]{1,0:T(8,128)(2,1)} %constant_dynamic-slice_fusion), channel_id=1, source_target_pairs={{0,1},{1,0},{2,3},{3,2},{4,5},{5,4},{6,7},{7,6},{8,9},{9,8},{10,11... | collective-permute-start | bytes 3145736 | tf_op jit(solution)/shard_map/ppermute | solution.py:162
  74.3 0.7 convert_element_type.78
  75.0 3.7 %collective-permute-start.4 = (bf16[8,8192]{1,0:T(8,128)(2,1)}, bf16[8,8192]{1,0:T(8,128)(2,1)}, u32[]{:S(2)}, u32[]{:S(2)}) collective-permute-start(bf16[8,8192]{1,0:T(8,128)(2,1)} %convert_element_type.78), channel_id=1, source_target_pairs={{0,64},{8,72},{16,80},{24,88},{32,96},{40,104},{48,112},{56,120},{... | collective-permute-start | bytes 393224 | tf_op jit(solution)/shard_map/ppermute | solution.py:127
  78.7 0.0 all-to-all-done.1
  78.8 0.0 copy-start.6
  78.8 0.1 convert_reduce_fusion.1
  78.8 0.0 copy-done.2
  78.8 0.1 subtract_convert_fusion
  78.9 16.0 %all-gather.2 = bf16[512,512]{1,0:T(8,128)(2,1)S(1)} all-gather(bf16[128,512]{1,0:T(8,128)(2,1)S(1)} %subtract_convert_fusion), channel_id=4, replica_groups={{0,2,4,6},{1,3,5,7},{8,10,12,14},{9,11,13,15},{16,18,20,22},{17,19,21,2..., dimensions={0}, use_global_device_ids=true | all-gather | bytes 655360 | tf_op jit(solution)/shard_map/all_gather | solution.py:171
  95.0 8.0 %collective-permute-start.3 = (bf16[512,512]{1,0:T(8,128)(2,1)S(1)}, bf16[512,512]{1,0:T(8,128)(2,1)S(1)}, u32[]{:S(2)}, u32[]{:S(2)}) collective-permute-start(bf16[512,512]{1,0:T(8,128)(2,1)S(1)} %all-gather.2), channel_id=1, source_target_pairs={{0,1},{1,0},{2,3},{3,2},{4,5},{5,4},{6,7},{7,6},{8,9},{9,8},{10,11... | collective-permute-start | bytes 1572872 | tf_op jit(solution)/shard_map/ppermute | solution.py:173
  102.9 0.0 collective-permute-done.4
  102.9 0.0 copy-done.3
  103.0 0.0 copy-done.5
  103.0 0.0 copy-done.6
  103.0 1.8 %fusion.5 = (bf16[1,8,8192]{2,1,0:T(8,128)(2,1)}, f32[8,8192]{1,0:T(8,128)}, f32[8,8192]{1,0:T(8,128)}) fusion(bf16[1,8,8192]{2,1,0:T(8,128)(2,1)S(1)} %copy-done.5, f32[8,8192]{1,0:T(8,128)S(1)} %copy-done.3, f32[8,8192]{1,0:T(8,128)S(1)} %convert_reduce_fusion, bf16[8,8192]{1,0:T(8,128)(2,1)} %collective-permute-done.4, f32[8,8192]{1,0:T(8,128)S(1)} %copy-done.6), kind=kLoop, calls=%fused_computation.13 | loop fusion | flops 851968 | bytes 1703936 | tf_op jit(solution)/shard_map/convert_element_type | solution.py:167
  104.8 0.7 fusion.2
  105.5 0.0 collective-permute-done.2
  105.5 0.0 collective-permute-done.3
  105.6 3.0 %fusion.1 = bf16[1,1024,512]{2,1,0:T(8,128)(2,1)} fusion(f32[1024,512]{1,0:T(8,128)S(1)} %fusion.2, bf16[512,1024]{1,0:T(8,128)(2,1)} %collective-permute-done.2, bf16[512,512]{1,0:T(8,128)(2,1)S(1)} %collective-permute-done.3, f32[1024]{0:T(1024)S(1)} %bitcast.36), kind=kOutput, calls=%fused_computation.4 | convolution fusion | flops 538443776 | bytes 4722688 | tf_op jit(solution)/shard_map/dot_general | solution.py:175
  (4 shorter events, 0.0 us)
Async XLA Ops:
  3.1 51.1 %all-to-all-start = ((bf16[4,128,2048]{2,1,0:T(8,128)(2,1)}), bf16[4,128,2048]{2,1,0:T(8,128)(2,1)S(1)}, u32[]{:S(2)}, u32[]{:S(2)}) async-start(bf16[4,128,2048]{2,1,0:T(8,128)(2,1)} %shard_map.102), calls=%async_computation | async-start | bytes 4194304 | tf_op jit(solution)/shard_map/all_to_all | solution.py:20
  15.8 14.4 %collective-permute-start = (bf16[8,8192]{1,0:T(8,128)(2,1)}, bf16[8,8192]{1,0:T(8,128)(2,1)S(1)}, u32[]{:S(2)}, u32[]{:S(2)}) collective-permute-start(bf16[8,8192]{1,0:T(8,128)(2,1)} %shard_map.103), channel_id=1, source_target_pairs={{0,32},{8,40},{16,48},{24,56},{32,0},{40,8},{48,16},{56,24},{64,96... | collective-permute-start | bytes 393224 | tf_op jit(solution)/shard_map/ppermute | solution.py:127
  23.2 5.6 %copy-start.1 = (bf16[1,128,8192]{2,1,0:T(8,128)(2,1)S(1)}, bf16[1,128,8192]{2,1,0:T(8,128)(2,1)}, u32[]{:S(2)}) copy-start(bf16[1,128,8192]{2,1,0:T(8,128)(2,1)} %param.7) | copy-start | bytes 6291460
  24.1 5.2 %copy-start.7 = (bf16[1,128,512]{2,1,0:T(8,128)(2,1)S(1)}, bf16[1,128,512]{2,1,0:T(8,128)(2,1)}, u32[]{:S(2)}) copy-start(bf16[1,128,512]{2,1,0:T(8,128)(2,1)} %param.10) | copy-start | bytes 393220
  24.1 6.0 %copy-start.4 = (bf16[8,8192]{1,0:T(8,128)(2,1)S(1)}, bf16[8,8192]{1,0:T(8,128)(2,1)}, u32[]{:S(2)}) copy-start(bf16[8,8192]{1,0:T(8,128)(2,1)} %shard_map.103) | copy-start | bytes 393220
  25.7 28.6 %collective-permute-start.1 = (bf16[1024,512]{1,0:T(8,128)(2,1)S(1)}, bf16[1024,512]{1,0:T(8,128)(2,1)}, u32[]{:S(2)}, u32[]{:S(2)}) collective-permute-start(bf16[1024,512]{1,0:T(8,128)(2,1)S(1)} %fusion.mine), channel_id=1, source_target_pairs={{0,1},{1,0},{2,3},{3,2},{4,5},{5,4},{6,7},{7,6},{8,9},{9,8},{10,11... | collective-permute-start | bytes 3145736 | tf_op jit(solution)/shard_map/ppermute | solution.py:146
  56.7 0.8 copy-start
  57.6 21.3 %copy-start.2 = (f32[128,512]{1,0:T(8,128)S(1)}, f32[128,512]{1,0:T(8,128)}, u32[]{:S(2)}) copy-start(f32[128,512]{1,0:T(8,128)} %convert_multiply_fusion.1) | copy-start | bytes 786436
  57.6 21.2 %all-to-all-start.1 = ((bf16[4,128,512]{2,1,0:T(8,128)(2,1)}), bf16[4,128,512]{2,1,0:T(8,128)(2,1)S(1)}, u32[]{:S(2)}, u32[]{:S(2)}) async-start(bf16[4,128,512]{2,1,0:T(8,128)(2,1)} %copy-done), calls=%async_computation.1 | async-start | bytes 1048576 | tf_op jit(solution)/shard_map/all_to_all | solution.py:20
  68.5 34.4 %copy-start.3 = (f32[8,8192]{1,0:T(8,128)S(1)}, f32[8,8192]{1,0:T(8,128)}, u32[]{:S(2)}) copy-start(f32[8,8192]{1,0:T(8,128)} %base.1) | copy-start | bytes 786436
  68.5 34.4 %copy-start.5 = (bf16[1,8,8192]{2,1,0:T(8,128)(2,1)S(1)}, bf16[1,8,8192]{2,1,0:T(8,128)(2,1)}, u32[]{:S(2)}) copy-start(bf16[1,8,8192]{2,1,0:T(8,128)(2,1)} %param.13) | copy-start | bytes 393220
  69.6 35.9 %collective-permute-start.2 = (bf16[512,1024]{1,0:T(8,128)(2,1)}, bf16[512,1024]{1,0:T(8,128)(2,1)}, u32[]{:S(2)}, u32[]{:S(2)}) collective-permute-start(bf16[512,1024]{1,0:T(8,128)(2,1)} %constant_dynamic-slice_fusion), channel_id=1, source_target_pairs={{0,1},{1,0},{2,3},{3,2},{4,5},{5,4},{6,7},{7,6},{8,9},{9,8},{10,11... | collective-permute-start | bytes 3145736 | tf_op jit(solution)/shard_map/ppermute | solution.py:162
  75.0 27.9 %collective-permute-start.4 = (bf16[8,8192]{1,0:T(8,128)(2,1)}, bf16[8,8192]{1,0:T(8,128)(2,1)}, u32[]{:S(2)}, u32[]{:S(2)}) collective-permute-start(bf16[8,8192]{1,0:T(8,128)(2,1)} %convert_element_type.78), channel_id=1, source_target_pairs={{0,64},{8,72},{16,80},{24,88},{32,96},{40,104},{48,112},{56,120},{... | collective-permute-start | bytes 393224 | tf_op jit(solution)/shard_map/ppermute | solution.py:127
  78.8 24.2 %copy-start.6 = (f32[8,8192]{1,0:T(8,128)S(1)}, f32[8,8192]{1,0:T(8,128)}, u32[]{:S(2)}) copy-start(f32[8,8192]{1,0:T(8,128)} %param.12) | copy-start | bytes 786436
  95.0 10.6 %collective-permute-start.3 = (bf16[512,512]{1,0:T(8,128)(2,1)S(1)}, bf16[512,512]{1,0:T(8,128)(2,1)S(1)}, u32[]{:S(2)}, u32[]{:S(2)}) collective-permute-start(bf16[512,512]{1,0:T(8,128)(2,1)S(1)} %all-gather.2), channel_id=1, source_target_pairs={{0,1},{1,0},{2,3},{3,2},{4,5},{5,4},{6,7},{7,6},{8,9},{9,8},{10,11... | collective-permute-start | bytes 1572872 | tf_op jit(solution)/shard_map/ppermute | solution.py:173

commit v3 on v2

--- a/solution.py
+++ b/solution.py
@@ -13,7 +13,7 @@
 SWAP = [(i, i ^ 1) for i in range(CHIPS * CORES)]
 F32 = jnp.float32
 BF16 = jnp.bfloat16
-LIMIT = 40 << 20
+GRAD_TILES = 4
 
 
 def chips_all_to_all(x):
@@ -55,36 +55,38 @@
     )(tok)
 
 
-def keys_kernel(core, x, mine, other, out):
+def keys_kernel(place, x, mine, other, offset, out):
     chips, rows, wide = x.shape
     depth, cols = mine.shape
-    near = x[:, :, pl.ds(pl.multiple_of(core[0] * depth, depth), depth)]
-    far = x[:, :, pl.ds(pl.multiple_of((1 - core[0]) * depth, depth), depth)]
+    near = x[:, :, pl.ds(pl.multiple_of(place[0] * depth, depth), depth)]
+    far = x[:, :, pl.ds(pl.multiple_of((1 - place[0]) * depth, depth), depth)]
     near = near.reshape(chips * rows, depth)
     far = far.reshape(chips * rows, depth)
     for at in range(0, cols, 256):
         part = pl.ds(at, 256)
         total = jnp.dot(near, mine[:, part], preferred_element_type=F32)
         total = total + jnp.dot(far, other[:, part], preferred_element_type=F32)
-        out[:, :, part] = total.astype(out.dtype).reshape(chips, rows, 256)
-
-
-def partial_keys(core, x, mine, other):
+        for z in range(chips):
+            own = (place[1] == z).astype(F32)
+            out[z, :, part] = (total[z * rows:(z + 1) * rows] - own * offset[:, part]).astype(out.dtype)
+
+
+def partial_keys(place, x, mine, other, offset):
     chips, rows, wide = x.shape
     cols = mine.shape[1]
     vmem = pl.BlockSpec(memory_space=pltpu.VMEM)
     return pl.pallas_call(
         keys_kernel,
-        in_specs=[pl.BlockSpec(memory_space=pltpu.SMEM), vmem, vmem, vmem],
+        in_specs=[pl.BlockSpec(memory_space=pltpu.SMEM), vmem, vmem, vmem, vmem],
         out_specs=vmem,
         out_shape=jax.ShapeDtypeStruct((chips, rows, cols), BF16),
-        compiler_params=pltpu.CompilerParams(vmem_limit_bytes=24 << 20),
+        compiler_params=pltpu.CompilerParams(vmem_limit_bytes=16 << 20),
         cost_estimate=pl.CostEstimate(
             flops=2 * chips * rows * wide * cols,
             bytes_accessed=2 * (chips * rows * (wide + cols) + wide * cols),
             transcendentals=0,
         ),
-    )(core, x, mine, other)
+    )(place, x, mine, other, offset)
 
 
 def quantize_kernel(base, params, out):
@@ -106,6 +108,42 @@
     )(base, params)
 
 
+def gradient_kernel(x, a, first, gain, out, held, go):
+    depth = x.shape[1]
+    tile = depth // GRAD_TILES
+    copies = []
+    for k in range(GRAD_TILES):
+        part = pl.ds(k * tile, tile)
+        total = first[part] + lax.dot_general(
+            x[:, part], a[...], (((0,), (0,)), ((), ())), preferred_element_type=F32
+        )
+        held[part] = (total * gain[part]).astype(held.dtype)
+        copy = pltpu.make_async_copy(held.at[part], out.at[part], go.at[k])
+        copy.start()
+        copies.append(copy)
+    for copy in copies:
+        copy.wait()
+
+
+def gradient(x, a, first, gain):
+    rows, depth = x.shape
+    cols = a.shape[1]
+    vmem = pl.BlockSpec(memory_space=pltpu.VMEM)
+    return pl.pallas_call(
+        gradient_kernel,
+        in_specs=[vmem] * 4,
+        out_specs=pl.BlockSpec(memory_space=pl.ANY),
+        out_shape=jax.ShapeDtypeStruct((depth, cols), BF16),
+        scratch_shapes=[pltpu.VMEM((depth, cols), BF16), pltpu.SemaphoreType.DMA((GRAD_TILES,))],
+        compiler_params=pltpu.CompilerParams(vmem_limit_bytes=16 << 20),
+        cost_estimate=pl.CostEstimate(
+            flops=2 * rows * depth * cols,
+            bytes_accessed=2 * rows * (depth + cols) + 6 * depth * cols,
+            transcendentals=0,
+        ),
+    )(x, a, first, gain)
+
+
 def fours_along_x(replicas):
     return [[r for r in range(replicas) if r % 16 == k] for k in range(16)]
 
@@ -134,12 +172,15 @@
     depth, cols = weights.shape
     me = lax.axis_index("fsdp")
     core = me % CORES
-    this_core = core[None].astype(jnp.int32)
+    place = jnp.stack([core, me // CORES]).astype(jnp.int32)
     wide = CORES * depth
     root = 1.0 / math.sqrt(rows * CHIPS * CORES)
     dims = (((0,), (0,)), ((), ()))
 
-    x = chips_all_to_all(split_features(tok))
+    pieces, outer_base, norm_gain = lax.optimization_barrier(
+        (split_features(tok), outer_base, norm_gain)
+    )
+    x = chips_all_to_all(pieces)
 
     gain = lax.dynamic_slice(norm_gain[0], (me * depth,), (depth,)).astype(F32)[:, None]
     mine = (weights.astype(F32) * gain).astype(BF16)
@@ -147,14 +188,13 @@
     values = tok.astype(F32)
     inv = lax.rsqrt(jnp.mean(values * values, axis=-1, keepdims=True) + 1e-05)
 
-    slope = root * inv
-    offset = key_target[0].astype(F32) * slope
-    slope = slope * inv
+    offset = key_target[0].astype(F32) / inv
+    slope = root * inv * inv
     summed = sum_of_sixteen(add_neighbour(quantize(outer_base, replica_params[0]), 4))
 
     x, summed, slope, offset = lax.optimization_barrier((x, summed, slope, offset))
 
-    part = partial_keys(this_core, x, mine, other)
+    part = partial_keys(place, x, mine, other, offset)
     parts = chips_all_to_all(part)
     x = x.reshape(CHIPS * rows, wide)
     x_mine = lax.dynamic_slice(x, (0, core * depth), (CHIPS * rows, depth))
@@ -167,13 +207,12 @@
     params_next = (0.5 * replica_params.astype(F32) + 0.5 * base_next[None]).astype(BF16)
 
     keys = jnp.sum(parts.astype(F32), axis=0)
-    cot = (keys * slope - offset).astype(BF16)
+    cot = (keys * slope).astype(BF16)
     cots = lax.all_gather(cot, "fsdp", axis=0, axis_index_groups=SAME)
     cots = cots.reshape(CHIPS * rows, cols)
     cots_other = lax.ppermute(cots, "fsdp", SWAP)
     one = lax.dot_general(x_mine, cots, dims, preferred_element_type=F32)
-    two = lax.dot_general(x_other, cots_other, dims, preferred_element_type=F32)
-    key_grad = ((one + two) * gain).astype(BF16)[None]
+    key_grad = gradient(x_other, cots_other, one, gain)[None]
     return (key_grad, base_next, momentum_next, params_next)
 
 

time: 110 us -> 109 us (level)
  matrix products: 3.71 us -> 0.74 us
  Pallas kernels: 6.76 us -> 9.48 us
  starting transfers between devices: 48.8 us -> 46.1 us
  other arithmetic: 6.5 us -> 8.37 us
    dot_general x1 -> x0, matrix products: 2.97 us -> none  [shards(): two = lax.dot_general(x_other, cots_other, dims, preferred_element_type=F32)]
    pallas_call x0 -> x1, Pallas kernels: none -> 2.74 us  [gradient(): pl.pallas_call(gradient_kernel, in_specs=[vmem] * 4, out_specs=pl.BlockSp...]
    all_to_all x2, starting transfers between devices: 21.8 us -> 19.8 us  [chips_all_to_all(): lax.all_to_all(x, 'fsdp', split_axis=0, concat_axis=0, axis_index_groups=...]
  transfers between devices with their start and end apart: 7 -> 7, of which waited for: 0 -> 0; matrix products, arithmetic and copies ran while one was open for 8% -> 10% of each run, Pallas kernels for 2% -> 2%
where the time goes in v3:
time: 109 us
  starting transfers between devices  46.1 us (42%)
  blocking collectives  40.8 us (37%)
  Pallas kernels  9.48 us (9%)
  other arithmetic  8.37 us (8%)
  local copies, waits for them, and re-layouts  2.12 us (2%)
    all_gather x2, blocking collectives, sum_of_sixteen(): lax.all_gather(x.astype(BF16), 'replica', axis=0, axis_index_groups=groups)  25 us
    all_to_all x2, starting transfers between devices, chips_all_to_all(): lax.all_to_all(x, 'fsdp', split_axis=0, concat_axis=0, axis_index_groups=...  19.8 us
    all_gather x1, blocking collectives, shards(): cots = lax.all_gather(cot, 'fsdp', axis=0, axis_index_groups=SAME)  15.8 us
    ppermute x2, starting transfers between devices, add_neighbour(): return x + lax.ppermute(x.astype(BF16), 'replica', pairs).astype(F32)  10.9 us
    ppermute x1, starting transfers between devices, shards(): cots_other = lax.ppermute(cots, 'fsdp', SWAP)  7.33 us
    ppermute x1, starting transfers between devices, shards(): x_other = lax.ppermute(x_send, 'fsdp', SWAP)  5 us
    ppermute x1, starting transfers between devices, shards(): other = lax.ppermute(mine, 'fsdp', SWAP)  3.14 us
    pallas_call x1, Pallas kernels, gradient(): pl.pallas_call(gradient_kernel, in_specs=[vmem] * 4, out_specs=pl.BlockSp...  2.74 us
  transfers between devices with their start and end apart: 7, of which 0 were waited for; matrix products, arithmetic and copies ran while one was open for 10% of the time, Pallas kernels for 2%

profile of v3, /device:TPU:1, one launch (start us, length us, event | category | flops | bytes accessed | tf_op | source)
XLA Modules:
  0.0 108.5 jit_solution(10421922843616009332)
XLA Ops:
  0.6 2.4 %shard_map.102 = bf16[4,128,2048]{2,1,0:T(8,128)(2,1)} custom-call(bf16[128,8192]{1,0:T(8,128)(2,1)} %bitcast.38), custom_call_target="tpu_custom_call" | custom-call | bytes 4194304 | tf_op jit(solution)/shard_map/pallas_call | solution.py:44
  3.1 10.9 %all-to-all-start = ((bf16[4,128,2048]{2,1,0:T(8,128)(2,1)}), bf16[4,128,2048]{2,1,0:T(8,128)(2,1)S(1)}, u32[]{:S(2)}, u32[]{:S(2)}) async-start(bf16[4,128,2048]{2,1,0:T(8,128)(2,1)} %shard_map.102), calls=%async_computation | async-start | bytes 4194304 | tf_op jit(solution)/shard_map/all_to_all | solution.py:20
  13.9 1.8 %shard_map.103 = bf16[8,8192]{1,0:T(8,128)(2,1)} custom-call(f32[8,8192]{1,0:T(8,128)} %base, bf16[8,8192]{1,0:T(8,128)(2,1)} %bitcast.42), custom_call_target="tpu_custom_call" | custom-call | flops 524288 | bytes 524288 | tf_op jit(solution)/shard_map/pallas_call | solution.py:102
  15.8 7.4 %collective-permute-start = (bf16[8,8192]{1,0:T(8,128)(2,1)}, bf16[8,8192]{1,0:T(8,128)(2,1)}, u32[]{:S(2)}, u32[]{:S(2)}) collective-permute-start(bf16[8,8192]{1,0:T(8,128)(2,1)} %shard_map.103), channel_id=1, source_target_pairs={{0,32},{8,40},{16,48},{24,56},{32,0},{40,8},{48,16},{56,24},{64,96... | collective-permute-start | bytes 393224 | tf_op jit(solution)/shard_map/ppermute | solution.py:165
  23.2 0.0 copy-start.1
  23.2 0.8 dynamic-slice_convert_fusion
  24.1 0.0 copy-start.5
  24.1 0.0 copy-start.3
  24.1 1.6 %fusion.mine = bf16[1024,512]{1,0:T(8,128)(2,1)S(1)} fusion(bf16[1,1024,512]{2,1,0:T(8,128)(2,1)} %param.9, f32[1024]{0:T(1024)S(1)} %bitcast.43), kind=kLoop, calls=%fused_computation.2 | loop fusion | flops 1572864 | bytes 2101248 | tf_op jit(solution)/shard_map/convert_element_type | solution.py:186
  25.6 3.1 %collective-permute-start.2 = (bf16[1024,512]{1,0:T(8,128)(2,1)S(1)}, bf16[1024,512]{1,0:T(8,128)(2,1)}, u32[]{:S(2)}, u32[]{:S(2)}) collective-permute-start(bf16[1024,512]{1,0:T(8,128)(2,1)S(1)} %fusion.mine), channel_id=1, source_target_pairs={{0,1},{1,0},{2,3},{3,2},{4,5},{5,4},{6,7},{7,6},{8,9},{9,8},{10,11... | collective-permute-start | bytes 3145736 | tf_op jit(solution)/shard_map/ppermute | solution.py:187
  28.8 0.0 copy-done.1
  28.8 0.5 multiply_reduce_fusion
  29.3 0.0 copy-done.5
  29.3 0.1 convert_divide_fusion.offset
  29.4 0.1 pad_add_fusion.place
  29.5 0.0 collective-permute-done
  29.5 0.0 copy-done.3
  29.5 0.9 add_convert_fusion
  30.5 11.4 %all-gather = bf16[32,8192]{1,0:T(8,128)(2,1)S(1)} all-gather(bf16[8,8192]{1,0:T(8,128)(2,1)S(1)} %add_convert_fusion), channel_id=2, replica_groups={{0,128,256,384},{8,136,264,392},{16,144,272,400},{24,152,280,408},{32,1..., dimensions={0}, use_global_device_ids=true | all-gather | bytes 655360 | tf_op jit(solution)/shard_map/all_gather | solution.py:158
  41.9 0.1 bitcast_reduce_fusion
  42.0 13.6 %all-gather.1 = bf16[32,8192]{1,0:T(8,128)(2,1)S(1)} all-gather(bf16[8,8192]{1,0:T(8,128)(2,1)S(1)} %bitcast_reduce_fusion), channel_id=3, replica_groups={{0,8,16,24},{32,40,48,56},{64,72,80,88},{96,104,112,120},{128,136,144,1..., dimensions={0}, use_global_device_ids=true | all-gather | bytes 655360 | tf_op jit(solution)/shard_map/all_gather | solution.py:158
  55.5 0.8 convert_reduce_fusion
  56.3 0.0 all-to-all-done.x
  56.3 0.0 collective-permute-done.2.other
  56.3 2.5 %shard_map.104 = bf16[4,128,512]{2,1,0:T(8,128)(2,1)S(1)} custom-call(s32[2]{0:T(128)S(1)} %pad_add_fusion.place, bf16[4,128,2048]{2,1,0:T(8,128)(2,1)S(1)} %all-to-all-done.x, bf16[1024,512]{1,0:T(8,128)(2,1)S(1)} %fusion.mine, bf16[1024,512]{1,0:T(8,128)(2,1)} %collective-permute-done.2.other, f32[128,512]{1,0:T(8,128)S(1)} %convert_divide_fusion.offset), custom_call_target="tpu_custom_call" | custom-call | flops 1073741824 | bytes 4718592 | tf_op jit(solution)/shard_map/pallas_call | solution.py:78
  58.8 0.0 copy-start
  58.8 0.8 copy-done
  59.6 8.9 %all-to-all-start.1 = ((bf16[4,128,512]{2,1,0:T(8,128)(2,1)}), bf16[4,128,512]{2,1,0:T(8,128)(2,1)S(1)}, u32[]{:S(2)}, u32[]{:S(2)}) async-start(bf16[4,128,512]{2,1,0:T(8,128)(2,1)} %copy-done), calls=%async_computation.1 | async-start | bytes 1048576 | tf_op jit(solution)/shard_map/all_to_all | solution.py:20
  68.5 0.7 fusion.8
  69.2 0.2 copy.13.gain
  69.5 0.0 copy-start.4
  69.5 1.1 constant_dynamic-slice_fusion
  70.5 5.0 %collective-permute-start.1 = (bf16[512,1024]{1,0:T(8,128)(2,1)}, bf16[512,1024]{1,0:T(8,128)(2,1)}, u32[]{:S(2)}, u32[]{:S(2)}) collective-permute-start(bf16[512,1024]{1,0:T(8,128)(2,1)} %constant_dynamic-slice_fusion), channel_id=1, source_target_pairs={{0,1},{1,0},{2,3},{3,2},{4,5},{5,4},{6,7},{7,6},{8,9},{9,8},{10,11... | collective-permute-start | bytes 3145736 | tf_op jit(solution)/shard_map/ppermute | solution.py:202
  75.5 0.0 copy-done.2
  75.6 0.7 convert_element_type.92
  76.2 3.4 %collective-permute-start.4 = (bf16[8,8192]{1,0:T(8,128)(2,1)}, bf16[8,8192]{1,0:T(8,128)(2,1)}, u32[]{:S(2)}, u32[]{:S(2)}) collective-permute-start(bf16[8,8192]{1,0:T(8,128)(2,1)} %convert_element_type.92), channel_id=1, source_target_pairs={{0,64},{8,72},{16,80},{24,88},{32,96},{40,104},{48,112},{56,120},{... | collective-permute-start | bytes 393224 | tf_op jit(solution)/shard_map/ppermute | solution.py:165
  79.7 0.0 all-to-all-done.1
  79.7 0.1 convert_reduce_fusion.1
  79.8 0.1 fusion.5
  79.8 15.8 %all_gather.20 = bf16[4,128,512]{2,1,0:T(8,128)(2,1)S(1)} all-gather(bf16[1,128,512]{2,1,0:T(8,128)(2,1)S(1)} %fusion.5), channel_id=1, replica_groups={{0,2,4,6},{1,3,5,7},{8,10,12,14},{9,11,13,15},{16,18,20,22},{17,19,21,2..., dimensions={0}, use_global_device_ids=true | all-gather | bytes 655360 | tf_op jit(solution)/shard_map/all_gather | solution.py:211
  95.7 7.3 %collective-permute-start.3 = (bf16[512,512]{1,0:T(8,128)(2,1)S(1)}, bf16[512,512]{1,0:T(8,128)(2,1)S(1)}, u32[]{:S(2)}, u32[]{:S(2)}) collective-permute-start(bf16[512,512]{1,0:T(8,128)(2,1)S(1)} %bitcast.39), channel_id=1, source_target_pairs={{0,1},{1,0},{2,3},{3,2},{4,5},{5,4},{6,7},{7,6},{8,9},{9,8},{10,11... | collective-permute-start | bytes 1572872 | tf_op jit(solution)/shard_map/ppermute | solution.py:213
  103.0 0.0 collective-permute-done.4
  103.0 0.0 copy-done.4
  103.0 2.0 %fusion.4 = (bf16[1,8,8192]{2,1,0:T(8,128)(2,1)}, f32[8,8192]{1,0:T(8,128)}, f32[8,8192]{1,0:T(8,128)}) fusion(bf16[1,8,8192]{2,1,0:T(8,128)(2,1)S(1)} %copy-done.4, f32[8,8192]{1,0:T(8,128)} %base, f32[8,8192]{1,0:T(8,128)S(1)} %copy-done.2, bf16[8,8192]{1,0:T(8,128)(2,1)} %collective-permute-done.4, f32[8,8192]{1,0:T(8,128)} %param.12), kind=kLoop, calls=%fused_computation.11 | loop fusion | flops 851968 | bytes 1703936 | tf_op jit(solution)/shard_map/convert_element_type | solution.py:207
  105.0 0.7 fusion.1.first
  105.8 0.0 collective-permute-done.1.x
  105.8 0.0 collective-permute-done.3.a
  105.8 2.7 %shard_map.105 = bf16[1024,512]{1,0:T(8,128)(2,1)} custom-call(bf16[512,1024]{1,0:T(8,128)(2,1)} %collective-permute-done.1.x, bf16[512,512]{1,0:T(8,128)(2,1)S(1)} %collective-permute-done.3.a, f32[1024,512]{1,0:T(8,128)S(1)} %fusion.1.first, f32[1024,1]{1,0:T(8,128)S(1)} %copy.13.gain), custom_call_target="tpu_custom_call" | custom-call | flops 536870912 | bytes 4718592 | tf_op jit(solution)/shard_map/pallas_call | solution.py:132
  (3 shorter events, 0.0 us)
Async XLA Ops:
  3.1 53.2 %all-to-all-start = ((bf16[4,128,2048]{2,1,0:T(8,128)(2,1)}), bf16[4,128,2048]{2,1,0:T(8,128)(2,1)S(1)}, u32[]{:S(2)}, u32[]{:S(2)}) async-start(bf16[4,128,2048]{2,1,0:T(8,128)(2,1)} %shard_map.102), calls=%async_computation | async-start | bytes 4194304 | tf_op jit(solution)/shard_map/all_to_all | solution.py:20
  15.8 13.8 %collective-permute-start = (bf16[8,8192]{1,0:T(8,128)(2,1)}, bf16[8,8192]{1,0:T(8,128)(2,1)}, u32[]{:S(2)}, u32[]{:S(2)}) collective-permute-start(bf16[8,8192]{1,0:T(8,128)(2,1)} %shard_map.103), channel_id=1, source_target_pairs={{0,32},{8,40},{16,48},{24,56},{32,0},{40,8},{48,16},{56,24},{64,96... | collective-permute-start | bytes 393224 | tf_op jit(solution)/shard_map/ppermute | solution.py:165
  23.2 5.6 %copy-start.1 = (bf16[1,128,8192]{2,1,0:T(8,128)(2,1)S(1)}, bf16[1,128,8192]{2,1,0:T(8,128)(2,1)}, u32[]{:S(2)}) copy-start(bf16[1,128,8192]{2,1,0:T(8,128)(2,1)} %param.7) | copy-start | bytes 6291460
  24.1 5.2 %copy-start.5 = (bf16[1,128,512]{2,1,0:T(8,128)(2,1)S(1)}, bf16[1,128,512]{2,1,0:T(8,128)(2,1)}, u32[]{:S(2)}) copy-start(bf16[1,128,512]{2,1,0:T(8,128)(2,1)} %param.10) | copy-start | bytes 393220
  24.1 5.4 %copy-start.3 = (bf16[8,8192]{1,0:T(8,128)(2,1)S(1)}, bf16[8,8192]{1,0:T(8,128)(2,1)}, u32[]{:S(2)}) copy-start(bf16[8,8192]{1,0:T(8,128)(2,1)} %shard_map.103) | copy-start | bytes 393220
  25.6 30.7 %collective-permute-start.2 = (bf16[1024,512]{1,0:T(8,128)(2,1)S(1)}, bf16[1024,512]{1,0:T(8,128)(2,1)}, u32[]{:S(2)}, u32[]{:S(2)}) collective-permute-start(bf16[1024,512]{1,0:T(8,128)(2,1)S(1)} %fusion.mine), channel_id=1, source_target_pairs={{0,1},{1,0},{2,3},{3,2},{4,5},{5,4},{6,7},{7,6},{8,9},{9,8},{10,11... | collective-permute-start | bytes 3145736 | tf_op jit(solution)/shard_map/ppermute | solution.py:187
  58.8 0.8 copy-start
  59.6 15.9 %copy-start.2 = (f32[8,8192]{1,0:T(8,128)S(1)}, f32[8,8192]{1,0:T(8,128)}, u32[]{:S(2)}) copy-start(f32[8,8192]{1,0:T(8,128)} %convert_reduce_fusion) | copy-start | bytes 786436
  59.6 20.1 %all-to-all-start.1 = ((bf16[4,128,512]{2,1,0:T(8,128)(2,1)}), bf16[4,128,512]{2,1,0:T(8,128)(2,1)S(1)}, u32[]{:S(2)}, u32[]{:S(2)}) async-start(bf16[4,128,512]{2,1,0:T(8,128)(2,1)} %copy-done), calls=%async_computation.1 | async-start | bytes 1048576 | tf_op jit(solution)/shard_map/all_to_all | solution.py:20
  69.5 33.6 %copy-start.4 = (bf16[1,8,8192]{2,1,0:T(8,128)(2,1)S(1)}, bf16[1,8,8192]{2,1,0:T(8,128)(2,1)}, u32[]{:S(2)}) copy-start(bf16[1,8,8192]{2,1,0:T(8,128)(2,1)} %param.13) | copy-start | bytes 393220
  70.5 35.2 %collective-permute-start.1 = (bf16[512,1024]{1,0:T(8,128)(2,1)}, bf16[512,1024]{1,0:T(8,128)(2,1)}, u32[]{:S(2)}, u32[]{:S(2)}) collective-permute-start(bf16[512,1024]{1,0:T(8,128)(2,1)} %constant_dynamic-slice_fusion), channel_id=1, source_target_pairs={{0,1},{1,0},{2,3},{3,2},{4,5},{5,4},{6,7},{7,6},{8,9},{9,8},{10,11... | collective-permute-start | bytes 3145736 | tf_op jit(solution)/shard_map/ppermute | solution.py:202
  76.2 26.8 %collective-permute-start.4 = (bf16[8,8192]{1,0:T(8,128)(2,1)}, bf16[8,8192]{1,0:T(8,128)(2,1)}, u32[]{:S(2)}, u32[]{:S(2)}) collective-permute-start(bf16[8,8192]{1,0:T(8,128)(2,1)} %convert_element_type.92), channel_id=1, source_target_pairs={{0,64},{8,72},{16,80},{24,88},{32,96},{40,104},{48,112},{56,120},{... | collective-permute-start | bytes 393224 | tf_op jit(solution)/shard_map/ppermute | solution.py:165
  95.7 10.1 %collective-permute-start.3 = (bf16[512,512]{1,0:T(8,128)(2,1)S(1)}, bf16[512,512]{1,0:T(8,128)(2,1)S(1)}, u32[]{:S(2)}, u32[]{:S(2)}) collective-permute-start(bf16[512,512]{1,0:T(8,128)(2,1)S(1)} %bitcast.39), channel_id=1, source_target_pairs={{0,1},{1,0},{2,3},{3,2},{4,5},{5,4},{6,7},{7,6},{8,9},{9,8},{10,11... | collective-permute-start | bytes 1572872 | tf_op jit(solution)/shard_map/ppermute | solution.py:213

commit v4 on v3

--- a/solution.py
+++ b/solution.py
@@ -108,14 +108,20 @@
     )(base, params)
 
 
-def gradient_kernel(x, a, first, gain, out, held, go):
+def gradient_kernel(x, a, first, gain, out, theirs, held, come, go):
     depth = x.shape[1]
     tile = depth // GRAD_TILES
     copies = []
+    ins = []
     for k in range(GRAD_TILES):
         part = pl.ds(k * tile, tile)
+        ins.append(pltpu.make_async_copy(x.at[:, part], theirs.at[:, part], come.at[k]))
+        ins[k].start()
+    for k in range(GRAD_TILES):
+        part = pl.ds(k * tile, tile)
+        ins[k].wait()
         total = first[part] + lax.dot_general(
-            x[:, part], a[...], (((0,), (0,)), ((), ())), preferred_element_type=F32
+            theirs[:, part], a[...], (((0,), (0,)), ((), ())), preferred_element_type=F32
         )
         held[part] = (total * gain[part]).astype(held.dtype)
         copy = pltpu.make_async_copy(held.at[part], out.at[part], go.at[k])
@@ -131,10 +137,15 @@
     vmem = pl.BlockSpec(memory_space=pltpu.VMEM)
     return pl.pallas_call(
         gradient_kernel,
-        in_specs=[vmem] * 4,
+        in_specs=[pl.BlockSpec(memory_space=pl.ANY)] + [vmem] * 3,
         out_specs=pl.BlockSpec(memory_space=pl.ANY),
         out_shape=jax.ShapeDtypeStruct((depth, cols), BF16),
-        scratch_shapes=[pltpu.VMEM((depth, cols), BF16), pltpu.SemaphoreType.DMA((GRAD_TILES,))],
+        scratch_shapes=[
+            pltpu.VMEM((rows, depth), BF16),
+            pltpu.VMEM((depth, cols), BF16),
+            pltpu.SemaphoreType.DMA((GRAD_TILES,)),
+            pltpu.SemaphoreType.DMA((GRAD_TILES,)),
+        ],
         compiler_params=pltpu.CompilerParams(vmem_limit_bytes=16 << 20),
         cost_estimate=pl.CostEstimate(
             flops=2 * rows * depth * cols,

time: 109 us -> 110 us (level)
  no operation moved by 1% of the time
where the time goes in v4:
time: 110 us; the launch traced here: 109 us
  starting transfers between devices  46.1 us (42%)
  blocking collectives  40.8 us (37%)
  Pallas kernels  9.8 us (9%)
  other arithmetic  8.37 us (8%)
  local copies, waits for them, and re-layouts  2.12 us (2%)
    all_gather x2, blocking collectives, sum_of_sixteen(): lax.all_gather(x.astype(BF16), 'replica', axis=0, axis_index_groups=groups)  25 us
    all_to_all x2, starting transfers between devices, chips_all_to_all(): lax.all_to_all(x, 'fsdp', split_axis=0, concat_axis=0, axis_index_groups=...  19.8 us
    all_gather x1, blocking collectives, shards(): cots = lax.all_gather(cot, 'fsdp', axis=0, axis_index_groups=SAME)  15.8 us
    ppermute x2, starting transfers between devices, add_neighbour(): return x + lax.ppermute(x.astype(BF16), 'replica', pairs).astype(F32)  10.9 us
    ppermute x1, starting transfers between devices, shards(): cots_other = lax.ppermute(cots, 'fsdp', SWAP)  7.33 us
    ppermute x1, starting transfers between devices, shards(): x_other = lax.ppermute(x_send, 'fsdp', SWAP)  5 us
    ppermute x1, starting transfers between devices, shards(): other = lax.ppermute(mine, 'fsdp', SWAP)  3.14 us
    pallas_call x1, Pallas kernels, gradient(): pl.pallas_call(gradient_kernel, in_specs=[pl.BlockSpec(memory_space=pl.AN...  3.06 us
  transfers between devices with their start and end apart: 7, of which 0 were waited for; matrix products, arithmetic and copies ran while one was open for 10% of the time, Pallas kernels for 2%

profile of v4, /device:TPU:1, one launch (start us, length us, event | category | flops | bytes accessed | tf_op | source)
XLA Modules:
  0.0 108.9 jit_solution(7828536791437299547)
XLA Ops:
  0.6 2.4 %shard_map.102 = bf16[4,128,2048]{2,1,0:T(8,128)(2,1)} custom-call(bf16[128,8192]{1,0:T(8,128)(2,1)} %bitcast.38), custom_call_target="tpu_custom_call" | custom-call | bytes 4194304 | tf_op jit(solution)/shard_map/pallas_call | solution.py:44
  3.1 10.9 %all-to-all-start = ((bf16[4,128,2048]{2,1,0:T(8,128)(2,1)}), bf16[4,128,2048]{2,1,0:T(8,128)(2,1)S(1)}, u32[]{:S(2)}, u32[]{:S(2)}) async-start(bf16[4,128,2048]{2,1,0:T(8,128)(2,1)} %shard_map.102), calls=%async_computation | async-start | bytes 4194304 | tf_op jit(solution)/shard_map/all_to_all | solution.py:20
  13.9 1.8 %shard_map.103 = bf16[8,8192]{1,0:T(8,128)(2,1)} custom-call(f32[8,8192]{1,0:T(8,128)} %base, bf16[8,8192]{1,0:T(8,128)(2,1)} %bitcast.42), custom_call_target="tpu_custom_call" | custom-call | flops 524288 | bytes 524288 | tf_op jit(solution)/shard_map/pallas_call | solution.py:102
  15.8 7.4 %collective-permute-start = (bf16[8,8192]{1,0:T(8,128)(2,1)}, bf16[8,8192]{1,0:T(8,128)(2,1)}, u32[]{:S(2)}, u32[]{:S(2)}) collective-permute-start(bf16[8,8192]{1,0:T(8,128)(2,1)} %shard_map.103), channel_id=1, source_target_pairs={{0,32},{8,40},{16,48},{24,56},{32,0},{40,8},{48,16},{56,24},{64,96... | collective-permute-start | bytes 393224 | tf_op jit(solution)/shard_map/ppermute | solution.py:176
  23.2 0.0 copy-start.1
  23.2 0.8 dynamic-slice_convert_fusion
  24.1 0.0 copy-start.5
  24.1 0.0 copy-start.3
  24.1 1.6 %fusion.mine = bf16[1024,512]{1,0:T(8,128)(2,1)S(1)} fusion(bf16[1,1024,512]{2,1,0:T(8,128)(2,1)} %param.9, f32[1024]{0:T(1024)S(1)} %bitcast.43), kind=kLoop, calls=%fused_computation.2 | loop fusion | flops 1572864 | bytes 2101248 | tf_op jit(solution)/shard_map/convert_element_type | solution.py:197
  25.6 3.1 %collective-permute-start.2 = (bf16[1024,512]{1,0:T(8,128)(2,1)S(1)}, bf16[1024,512]{1,0:T(8,128)(2,1)}, u32[]{:S(2)}, u32[]{:S(2)}) collective-permute-start(bf16[1024,512]{1,0:T(8,128)(2,1)S(1)} %fusion.mine), channel_id=1, source_target_pairs={{0,1},{1,0},{2,3},{3,2},{4,5},{5,4},{6,7},{7,6},{8,9},{9,8},{10,11... | collective-permute-start | bytes 3145736 | tf_op jit(solution)/shard_map/ppermute | solution.py:198
  28.8 0.0 copy-done.1
  28.8 0.5 multiply_reduce_fusion
  29.3 0.0 copy-done.5
  29.3 0.1 convert_divide_fusion.offset
  29.4 0.1 pad_add_fusion.place
  29.5 0.0 collective-permute-done
  29.5 0.0 copy-done.3
  29.5 0.9 add_convert_fusion
  30.5 11.4 %all-gather = bf16[32,8192]{1,0:T(8,128)(2,1)S(1)} all-gather(bf16[8,8192]{1,0:T(8,128)(2,1)S(1)} %add_convert_fusion), channel_id=2, replica_groups={{0,128,256,384},{8,136,264,392},{16,144,272,400},{24,152,280,408},{32,1..., dimensions={0}, use_global_device_ids=true | all-gather | bytes 655360 | tf_op jit(solution)/shard_map/all_gather | solution.py:169
  41.9 0.1 bitcast_reduce_fusion
  42.0 13.6 %all-gather.1 = bf16[32,8192]{1,0:T(8,128)(2,1)S(1)} all-gather(bf16[8,8192]{1,0:T(8,128)(2,1)S(1)} %bitcast_reduce_fusion), channel_id=3, replica_groups={{0,8,16,24},{32,40,48,56},{64,72,80,88},{96,104,112,120},{128,136,144,1..., dimensions={0}, use_global_device_ids=true | all-gather | bytes 655360 | tf_op jit(solution)/shard_map/all_gather | solution.py:169
  55.5 0.8 convert_reduce_fusion
  56.3 0.0 all-to-all-done.x
  56.3 0.0 collective-permute-done.2.other
  56.3 2.5 %shard_map.104 = bf16[4,128,512]{2,1,0:T(8,128)(2,1)S(1)} custom-call(s32[2]{0:T(128)S(1)} %pad_add_fusion.place, bf16[4,128,2048]{2,1,0:T(8,128)(2,1)S(1)} %all-to-all-done.x, bf16[1024,512]{1,0:T(8,128)(2,1)S(1)} %fusion.mine, bf16[1024,512]{1,0:T(8,128)(2,1)} %collective-permute-done.2.other, f32[128,512]{1,0:T(8,128)S(1)} %convert_divide_fusion.offset), custom_call_target="tpu_custom_call" | custom-call | flops 1073741824 | bytes 4718592 | tf_op jit(solution)/shard_map/pallas_call | solution.py:78
  58.8 0.0 copy-start
  58.8 0.8 copy-done
  59.6 8.9 %all-to-all-start.1 = ((bf16[4,128,512]{2,1,0:T(8,128)(2,1)}), bf16[4,128,512]{2,1,0:T(8,128)(2,1)S(1)}, u32[]{:S(2)}, u32[]{:S(2)}) async-start(bf16[4,128,512]{2,1,0:T(8,128)(2,1)} %copy-done), calls=%async_computation.1 | async-start | bytes 1048576 | tf_op jit(solution)/shard_map/all_to_all | solution.py:20
  68.5 0.7 fusion.8
  69.2 0.2 copy.13.gain
  69.5 0.0 copy-start.4
  69.5 1.1 constant_dynamic-slice_fusion
  70.5 5.0 %collective-permute-start.1 = (bf16[512,1024]{1,0:T(8,128)(2,1)}, bf16[512,1024]{1,0:T(8,128)(2,1)}, u32[]{:S(2)}, u32[]{:S(2)}) collective-permute-start(bf16[512,1024]{1,0:T(8,128)(2,1)} %constant_dynamic-slice_fusion), channel_id=1, source_target_pairs={{0,1},{1,0},{2,3},{3,2},{4,5},{5,4},{6,7},{7,6},{8,9},{9,8},{10,11... | collective-permute-start | bytes 3145736 | tf_op jit(solution)/shard_map/ppermute | solution.py:213
  75.5 0.0 copy-done.2
  75.6 0.7 convert_element_type.92
  76.2 3.4 %collective-permute-start.4 = (bf16[8,8192]{1,0:T(8,128)(2,1)}, bf16[8,8192]{1,0:T(8,128)(2,1)}, u32[]{:S(2)}, u32[]{:S(2)}) collective-permute-start(bf16[8,8192]{1,0:T(8,128)(2,1)} %convert_element_type.92), channel_id=1, source_target_pairs={{0,64},{8,72},{16,80},{24,88},{32,96},{40,104},{48,112},{56,120},{... | collective-permute-start | bytes 393224 | tf_op jit(solution)/shard_map/ppermute | solution.py:176
  79.7 0.0 all-to-all-done.1
  79.7 0.1 convert_reduce_fusion.1
  79.8 0.1 fusion.5
  79.8 15.8 %all_gather.20 = bf16[4,128,512]{2,1,0:T(8,128)(2,1)S(1)} all-gather(bf16[1,128,512]{2,1,0:T(8,128)(2,1)S(1)} %fusion.5), channel_id=1, replica_groups={{0,2,4,6},{1,3,5,7},{8,10,12,14},{9,11,13,15},{16,18,20,22},{17,19,21,2..., dimensions={0}, use_global_device_ids=true | all-gather | bytes 655360 | tf_op jit(solution)/shard_map/all_gather | solution.py:222
  95.7 7.3 %collective-permute-start.3 = (bf16[512,512]{1,0:T(8,128)(2,1)S(1)}, bf16[512,512]{1,0:T(8,128)(2,1)S(1)}, u32[]{:S(2)}, u32[]{:S(2)}) collective-permute-start(bf16[512,512]{1,0:T(8,128)(2,1)S(1)} %bitcast.39), channel_id=1, source_target_pairs={{0,1},{1,0},{2,3},{3,2},{4,5},{5,4},{6,7},{7,6},{8,9},{9,8},{10,11... | collective-permute-start | bytes 1572872 | tf_op jit(solution)/shard_map/ppermute | solution.py:224
  103.0 0.0 collective-permute-done.4
  103.0 0.0 copy-done.4
  103.0 2.0 %fusion.4 = (bf16[1,8,8192]{2,1,0:T(8,128)(2,1)}, f32[8,8192]{1,0:T(8,128)}, f32[8,8192]{1,0:T(8,128)}) fusion(bf16[1,8,8192]{2,1,0:T(8,128)(2,1)S(1)} %copy-done.4, f32[8,8192]{1,0:T(8,128)} %base, f32[8,8192]{1,0:T(8,128)S(1)} %copy-done.2, bf16[8,8192]{1,0:T(8,128)(2,1)} %collective-permute-done.4, f32[8,8192]{1,0:T(8,128)} %param.12), kind=kLoop, calls=%fused_computation.11 | loop fusion | flops 851968 | bytes 1703936 | tf_op jit(solution)/shard_map/convert_element_type | solution.py:218
  105.0 0.7 fusion.1.first
  105.8 0.0 collective-permute-done.1.x
  105.8 0.0 collective-permute-done.3.a
  105.8 3.1 %shard_map.105 = bf16[1024,512]{1,0:T(8,128)(2,1)} custom-call(bf16[512,1024]{1,0:T(8,128)(2,1)} %collective-permute-done.1.x, bf16[512,512]{1,0:T(8,128)(2,1)S(1)} %collective-permute-done.3.a, f32[1024,512]{1,0:T(8,128)S(1)} %fusion.1.first, f32[1024,1]{1,0:T(8,128)S(1)} %copy.13.gain), custom_call_target="tpu_custom_call" | custom-call | flops 536870912 | bytes 4718592 | tf_op jit(solution)/shard_map/pallas_call | solution.py:138
  (3 shorter events, 0.0 us)
Async XLA Ops:
  3.1 53.2 %all-to-all-start = ((bf16[4,128,2048]{2,1,0:T(8,128)(2,1)}), bf16[4,128,2048]{2,1,0:T(8,128)(2,1)S(1)}, u32[]{:S(2)}, u32[]{:S(2)}) async-start(bf16[4,128,2048]{2,1,0:T(8,128)(2,1)} %shard_map.102), calls=%async_computation | async-start | bytes 4194304 | tf_op jit(solution)/shard_map/all_to_all | solution.py:20
  15.8 13.8 %collective-permute-start = (bf16[8,8192]{1,0:T(8,128)(2,1)}, bf16[8,8192]{1,0:T(8,128)(2,1)}, u32[]{:S(2)}, u32[]{:S(2)}) collective-permute-start(bf16[8,8192]{1,0:T(8,128)(2,1)} %shard_map.103), channel_id=1, source_target_pairs={{0,32},{8,40},{16,48},{24,56},{32,0},{40,8},{48,16},{56,24},{64,96... | collective-permute-start | bytes 393224 | tf_op jit(solution)/shard_map/ppermute | solution.py:176
  23.2 5.6 %copy-start.1 = (bf16[1,128,8192]{2,1,0:T(8,128)(2,1)S(1)}, bf16[1,128,8192]{2,1,0:T(8,128)(2,1)}, u32[]{:S(2)}) copy-start(bf16[1,128,8192]{2,1,0:T(8,128)(2,1)} %param.7) | copy-start | bytes 6291460
  24.1 5.2 %copy-start.5 = (bf16[1,128,512]{2,1,0:T(8,128)(2,1)S(1)}, bf16[1,128,512]{2,1,0:T(8,128)(2,1)}, u32[]{:S(2)}) copy-start(bf16[1,128,512]{2,1,0:T(8,128)(2,1)} %param.10) | copy-start | bytes 393220
  24.1 5.4 %copy-start.3 = (bf16[8,8192]{1,0:T(8,128)(2,1)S(1)}, bf16[8,8192]{1,0:T(8,128)(2,1)}, u32[]{:S(2)}) copy-start(bf16[8,8192]{1,0:T(8,128)(2,1)} %shard_map.103) | copy-start | bytes 393220
  25.6 30.7 %collective-permute-start.2 = (bf16[1024,512]{1,0:T(8,128)(2,1)S(1)}, bf16[1024,512]{1,0:T(8,128)(2,1)}, u32[]{:S(2)}, u32[]{:S(2)}) collective-permute-start(bf16[1024,512]{1,0:T(8,128)(2,1)S(1)} %fusion.mine), channel_id=1, source_target_pairs={{0,1},{1,0},{2,3},{3,2},{4,5},{5,4},{6,7},{7,6},{8,9},{9,8},{10,11... | collective-permute-start | bytes 3145736 | tf_op jit(solution)/shard_map/ppermute | solution.py:198
  58.8 0.8 copy-start
  59.6 15.9 %copy-start.2 = (f32[8,8192]{1,0:T(8,128)S(1)}, f32[8,8192]{1,0:T(8,128)}, u32[]{:S(2)}) copy-start(f32[8,8192]{1,0:T(8,128)} %convert_reduce_fusion) | copy-start | bytes 786436
  59.6 20.1 %all-to-all-start.1 = ((bf16[4,128,512]{2,1,0:T(8,128)(2,1)}), bf16[4,128,512]{2,1,0:T(8,128)(2,1)S(1)}, u32[]{:S(2)}, u32[]{:S(2)}) async-start(bf16[4,128,512]{2,1,0:T(8,128)(2,1)} %copy-done), calls=%async_computation.1 | async-start | bytes 1048576 | tf_op jit(solution)/shard_map/all_to_all | solution.py:20
  69.5 33.6 %copy-start.4 = (bf16[1,8,8192]{2,1,0:T(8,128)(2,1)S(1)}, bf16[1,8,8192]{2,1,0:T(8,128)(2,1)}, u32[]{:S(2)}) copy-start(bf16[1,8,8192]{2,1,0:T(8,128)(2,1)} %param.13) | copy-start | bytes 393220
  70.5 35.2 %collective-permute-start.1 = (bf16[512,1024]{1,0:T(8,128)(2,1)}, bf16[512,1024]{1,0:T(8,128)(2,1)}, u32[]{:S(2)}, u32[]{:S(2)}) collective-permute-start(bf16[512,1024]{1,0:T(8,128)(2,1)} %constant_dynamic-slice_fusion), channel_id=1, source_target_pairs={{0,1},{1,0},{2,3},{3,2},{4,5},{5,4},{6,7},{7,6},{8,9},{9,8},{10,11... | collective-permute-start | bytes 3145736 | tf_op jit(solution)/shard_map/ppermute | solution.py:213
  76.2 26.8 %collective-permute-start.4 = (bf16[8,8192]{1,0:T(8,128)(2,1)}, bf16[8,8192]{1,0:T(8,128)(2,1)}, u32[]{:S(2)}, u32[]{:S(2)}) collective-permute-start(bf16[8,8192]{1,0:T(8,128)(2,1)} %convert_element_type.92), channel_id=1, source_target_pairs={{0,64},{8,72},{16,80},{24,88},{32,96},{40,104},{48,112},{56,120},{... | collective-permute-start | bytes 393224 | tf_op jit(solution)/shard_map/ppermute | solution.py:176
  95.7 10.1 %collective-permute-start.3 = (bf16[512,512]{1,0:T(8,128)(2,1)S(1)}, bf16[512,512]{1,0:T(8,128)(2,1)S(1)}, u32[]{:S(2)}, u32[]{:S(2)}) collective-permute-start(bf16[512,512]{1,0:T(8,128)(2,1)S(1)} %bitcast.39), channel_id=1, source_target_pairs={{0,1},{1,0},{2,3},{3,2},{4,5},{5,4},{6,7},{7,6},{8,9},{9,8},{10,11... | collective-permute-start | bytes 1572872 | tf_op jit(solution)/shard_map/ppermute | solution.py:224

commit v5 on v3

--- a/solution.py
+++ b/solution.py
@@ -13,7 +13,7 @@
 SWAP = [(i, i ^ 1) for i in range(CHIPS * CORES)]
 F32 = jnp.float32
 BF16 = jnp.bfloat16
-GRAD_TILES = 4
+GRAD_TILES = 2
 
 
 def chips_all_to_all(x):

time: 109 us -> 109 us (level)
  no operation moved by 1% of the time
where the time goes in v5:
time: 109 us
  starting transfers between devices  46.1 us (42%)
  blocking collectives  40.8 us (37%)
  Pallas kernels  9.55 us (9%)
  other arithmetic  8.37 us (8%)
  local copies, waits for them, and re-layouts  2.12 us (2%)
    all_gather x2, blocking collectives, sum_of_sixteen(): lax.all_gather(x.astype(BF16), 'replica', axis=0, axis_index_groups=groups)  25 us
    all_to_all x2, starting transfers between devices, chips_all_to_all(): lax.all_to_all(x, 'fsdp', split_axis=0, concat_axis=0, axis_index_groups=...  19.8 us
    all_gather x1, blocking collectives, shards(): cots = lax.all_gather(cot, 'fsdp', axis=0, axis_index_groups=SAME)  15.8 us
    ppermute x2, starting transfers between devices, add_neighbour(): return x + lax.ppermute(x.astype(BF16), 'replica', pairs).astype(F32)  10.9 us
    ppermute x1, starting transfers between devices, shards(): cots_other = lax.ppermute(cots, 'fsdp', SWAP)  7.33 us
    ppermute x1, starting transfers between devices, shards(): x_other = lax.ppermute(x_send, 'fsdp', SWAP)  5 us
    ppermute x1, starting transfers between devices, shards(): other = lax.ppermute(mine, 'fsdp', SWAP)  3.14 us
    pallas_call x1, Pallas kernels, gradient(): pl.pallas_call(gradient_kernel, in_specs=[vmem] * 4, out_specs=pl.BlockSp...  2.8 us
  transfers between devices with their start and end apart: 7, of which 0 were waited for; matrix products, arithmetic and copies ran while one was open for 10% of the time, Pallas kernels for 2%

profile of v5, /device:TPU:1, one launch (start us, length us, event | category | flops | bytes accessed | tf_op | source)
XLA Modules:
  0.0 108.6 jit_solution(5815801483240859386)
XLA Ops:
  0.6 2.4 %shard_map.102 = bf16[4,128,2048]{2,1,0:T(8,128)(2,1)} custom-call(bf16[128,8192]{1,0:T(8,128)(2,1)} %bitcast.38), custom_call_target="tpu_custom_call" | custom-call | bytes 4194304 | tf_op jit(solution)/shard_map/pallas_call | solution.py:44
  3.1 10.9 %all-to-all-start = ((bf16[4,128,2048]{2,1,0:T(8,128)(2,1)}), bf16[4,128,2048]{2,1,0:T(8,128)(2,1)S(1)}, u32[]{:S(2)}, u32[]{:S(2)}) async-start(bf16[4,128,2048]{2,1,0:T(8,128)(2,1)} %shard_map.102), calls=%async_computation | async-start | bytes 4194304 | tf_op jit(solution)/shard_map/all_to_all | solution.py:20
  13.9 1.8 %shard_map.103 = bf16[8,8192]{1,0:T(8,128)(2,1)} custom-call(f32[8,8192]{1,0:T(8,128)} %base, bf16[8,8192]{1,0:T(8,128)(2,1)} %bitcast.42), custom_call_target="tpu_custom_call" | custom-call | flops 524288 | bytes 524288 | tf_op jit(solution)/shard_map/pallas_call | solution.py:102
  15.8 7.4 %collective-permute-start = (bf16[8,8192]{1,0:T(8,128)(2,1)}, bf16[8,8192]{1,0:T(8,128)(2,1)}, u32[]{:S(2)}, u32[]{:S(2)}) collective-permute-start(bf16[8,8192]{1,0:T(8,128)(2,1)} %shard_map.103), channel_id=1, source_target_pairs={{0,32},{8,40},{16,48},{24,56},{32,0},{40,8},{48,16},{56,24},{64,96... | collective-permute-start | bytes 393224 | tf_op jit(solution)/shard_map/ppermute | solution.py:165
  23.2 0.0 copy-start.1
  23.2 0.8 dynamic-slice_convert_fusion
  24.1 0.0 copy-start.5
  24.1 0.0 copy-start.3
  24.1 1.6 %fusion.mine = bf16[1024,512]{1,0:T(8,128)(2,1)S(1)} fusion(bf16[1,1024,512]{2,1,0:T(8,128)(2,1)} %param.9, f32[1024]{0:T(1024)S(1)} %bitcast.43), kind=kLoop, calls=%fused_computation.2 | loop fusion | flops 1572864 | bytes 2101248 | tf_op jit(solution)/shard_map/convert_element_type | solution.py:186
  25.6 3.1 %collective-permute-start.2 = (bf16[1024,512]{1,0:T(8,128)(2,1)S(1)}, bf16[1024,512]{1,0:T(8,128)(2,1)}, u32[]{:S(2)}, u32[]{:S(2)}) collective-permute-start(bf16[1024,512]{1,0:T(8,128)(2,1)S(1)} %fusion.mine), channel_id=1, source_target_pairs={{0,1},{1,0},{2,3},{3,2},{4,5},{5,4},{6,7},{7,6},{8,9},{9,8},{10,11... | collective-permute-start | bytes 3145736 | tf_op jit(solution)/shard_map/ppermute | solution.py:187
  28.8 0.0 copy-done.1
  28.8 0.5 multiply_reduce_fusion
  29.3 0.0 copy-done.5
  29.3 0.1 convert_divide_fusion.offset
  29.4 0.1 pad_add_fusion.place
  29.5 0.0 collective-permute-done
  29.5 0.0 copy-done.3
  29.5 0.9 add_convert_fusion
  30.5 11.4 %all-gather = bf16[32,8192]{1,0:T(8,128)(2,1)S(1)} all-gather(bf16[8,8192]{1,0:T(8,128)(2,1)S(1)} %add_convert_fusion), channel_id=2, replica_groups={{0,128,256,384},{8,136,264,392},{16,144,272,400},{24,152,280,408},{32,1..., dimensions={0}, use_global_device_ids=true | all-gather | bytes 655360 | tf_op jit(solution)/shard_map/all_gather | solution.py:158
  41.9 0.1 bitcast_reduce_fusion
  42.0 13.6 %all-gather.1 = bf16[32,8192]{1,0:T(8,128)(2,1)S(1)} all-gather(bf16[8,8192]{1,0:T(8,128)(2,1)S(1)} %bitcast_reduce_fusion), channel_id=3, replica_groups={{0,8,16,24},{32,40,48,56},{64,72,80,88},{96,104,112,120},{128,136,144,1..., dimensions={0}, use_global_device_ids=true | all-gather | bytes 655360 | tf_op jit(solution)/shard_map/all_gather | solution.py:158
  55.5 0.8 convert_reduce_fusion
  56.3 0.0 all-to-all-done.x
  56.3 0.0 collective-permute-done.2.other
  56.3 2.5 %shard_map.104 = bf16[4,128,512]{2,1,0:T(8,128)(2,1)S(1)} custom-call(s32[2]{0:T(128)S(1)} %pad_add_fusion.place, bf16[4,128,2048]{2,1,0:T(8,128)(2,1)S(1)} %all-to-all-done.x, bf16[1024,512]{1,0:T(8,128)(2,1)S(1)} %fusion.mine, bf16[1024,512]{1,0:T(8,128)(2,1)} %collective-permute-done.2.other, f32[128,512]{1,0:T(8,128)S(1)} %convert_divide_fusion.offset), custom_call_target="tpu_custom_call" | custom-call | flops 1073741824 | bytes 4718592 | tf_op jit(solution)/shard_map/pallas_call | solution.py:78
  58.8 0.0 copy-start
  58.8 0.8 copy-done
  59.6 8.9 %all-to-all-start.1 = ((bf16[4,128,512]{2,1,0:T(8,128)(2,1)}), bf16[4,128,512]{2,1,0:T(8,128)(2,1)S(1)}, u32[]{:S(2)}, u32[]{:S(2)}) async-start(bf16[4,128,512]{2,1,0:T(8,128)(2,1)} %copy-done), calls=%async_computation.1 | async-start | bytes 1048576 | tf_op jit(solution)/shard_map/all_to_all | solution.py:20
  68.5 0.7 fusion.8
  69.2 0.2 copy.13.gain
  69.5 0.0 copy-start.4
  69.5 1.1 constant_dynamic-slice_fusion
  70.5 5.0 %collective-permute-start.1 = (bf16[512,1024]{1,0:T(8,128)(2,1)}, bf16[512,1024]{1,0:T(8,128)(2,1)}, u32[]{:S(2)}, u32[]{:S(2)}) collective-permute-start(bf16[512,1024]{1,0:T(8,128)(2,1)} %constant_dynamic-slice_fusion), channel_id=1, source_target_pairs={{0,1},{1,0},{2,3},{3,2},{4,5},{5,4},{6,7},{7,6},{8,9},{9,8},{10,11... | collective-permute-start | bytes 3145736 | tf_op jit(solution)/shard_map/ppermute | solution.py:202
  75.5 0.0 copy-done.2
  75.6 0.7 convert_element_type.92
  76.2 3.4 %collective-permute-start.4 = (bf16[8,8192]{1,0:T(8,128)(2,1)}, bf16[8,8192]{1,0:T(8,128)(2,1)}, u32[]{:S(2)}, u32[]{:S(2)}) collective-permute-start(bf16[8,8192]{1,0:T(8,128)(2,1)} %convert_element_type.92), channel_id=1, source_target_pairs={{0,64},{8,72},{16,80},{24,88},{32,96},{40,104},{48,112},{56,120},{... | collective-permute-start | bytes 393224 | tf_op jit(solution)/shard_map/ppermute | solution.py:165
  79.7 0.0 all-to-all-done.1
  79.7 0.1 convert_reduce_fusion.1
  79.8 0.1 fusion.5
  79.8 15.8 %all_gather.20 = bf16[4,128,512]{2,1,0:T(8,128)(2,1)S(1)} all-gather(bf16[1,128,512]{2,1,0:T(8,128)(2,1)S(1)} %fusion.5), channel_id=1, replica_groups={{0,2,4,6},{1,3,5,7},{8,10,12,14},{9,11,13,15},{16,18,20,22},{17,19,21,2..., dimensions={0}, use_global_device_ids=true | all-gather | bytes 655360 | tf_op jit(solution)/shard_map/all_gather | solution.py:211
  95.7 7.3 %collective-permute-start.3 = (bf16[512,512]{1,0:T(8,128)(2,1)S(1)}, bf16[512,512]{1,0:T(8,128)(2,1)S(1)}, u32[]{:S(2)}, u32[]{:S(2)}) collective-permute-start(bf16[512,512]{1,0:T(8,128)(2,1)S(1)} %bitcast.39), channel_id=1, source_target_pairs={{0,1},{1,0},{2,3},{3,2},{4,5},{5,4},{6,7},{7,6},{8,9},{9,8},{10,11... | collective-permute-start | bytes 1572872 | tf_op jit(solution)/shard_map/ppermute | solution.py:213
  103.0 0.0 collective-permute-done.4
  103.0 0.0 copy-done.4
  103.0 2.0 %fusion.4 = (bf16[1,8,8192]{2,1,0:T(8,128)(2,1)}, f32[8,8192]{1,0:T(8,128)}, f32[8,8192]{1,0:T(8,128)}) fusion(bf16[1,8,8192]{2,1,0:T(8,128)(2,1)S(1)} %copy-done.4, f32[8,8192]{1,0:T(8,128)} %base, f32[8,8192]{1,0:T(8,128)S(1)} %copy-done.2, bf16[8,8192]{1,0:T(8,128)(2,1)} %collective-permute-done.4, f32[8,8192]{1,0:T(8,128)} %param.12), kind=kLoop, calls=%fused_computation.11 | loop fusion | flops 851968 | bytes 1703936 | tf_op jit(solution)/shard_map/convert_element_type | solution.py:207
  105.0 0.7 fusion.1.first
  105.8 0.0 collective-permute-done.1.x
  105.8 0.0 collective-permute-done.3.a
  105.8 2.8 %shard_map.105 = bf16[1024,512]{1,0:T(8,128)(2,1)} custom-call(bf16[512,1024]{1,0:T(8,128)(2,1)} %collective-permute-done.1.x, bf16[512,512]{1,0:T(8,128)(2,1)S(1)} %collective-permute-done.3.a, f32[1024,512]{1,0:T(8,128)S(1)} %fusion.1.first, f32[1024,1]{1,0:T(8,128)S(1)} %copy.13.gain), custom_call_target="tpu_custom_call" | custom-call | flops 536870912 | bytes 4718592 | tf_op jit(solution)/shard_map/pallas_call | solution.py:132
  (3 shorter events, 0.0 us)
Async XLA Ops:
  3.1 53.2 %all-to-all-start = ((bf16[4,128,2048]{2,1,0:T(8,128)(2,1)}), bf16[4,128,2048]{2,1,0:T(8,128)(2,1)S(1)}, u32[]{:S(2)}, u32[]{:S(2)}) async-start(bf16[4,128,2048]{2,1,0:T(8,128)(2,1)} %shard_map.102), calls=%async_computation | async-start | bytes 4194304 | tf_op jit(solution)/shard_map/all_to_all | solution.py:20
  15.8 13.8 %collective-permute-start = (bf16[8,8192]{1,0:T(8,128)(2,1)}, bf16[8,8192]{1,0:T(8,128)(2,1)}, u32[]{:S(2)}, u32[]{:S(2)}) collective-permute-start(bf16[8,8192]{1,0:T(8,128)(2,1)} %shard_map.103), channel_id=1, source_target_pairs={{0,32},{8,40},{16,48},{24,56},{32,0},{40,8},{48,16},{56,24},{64,96... | collective-permute-start | bytes 393224 | tf_op jit(solution)/shard_map/ppermute | solution.py:165
  23.2 5.6 %copy-start.1 = (bf16[1,128,8192]{2,1,0:T(8,128)(2,1)S(1)}, bf16[1,128,8192]{2,1,0:T(8,128)(2,1)}, u32[]{:S(2)}) copy-start(bf16[1,128,8192]{2,1,0:T(8,128)(2,1)} %param.7) | copy-start | bytes 6291460
  24.1 5.2 %copy-start.5 = (bf16[1,128,512]{2,1,0:T(8,128)(2,1)S(1)}, bf16[1,128,512]{2,1,0:T(8,128)(2,1)}, u32[]{:S(2)}) copy-start(bf16[1,128,512]{2,1,0:T(8,128)(2,1)} %param.10) | copy-start | bytes 393220
  24.1 5.4 %copy-start.3 = (bf16[8,8192]{1,0:T(8,128)(2,1)S(1)}, bf16[8,8192]{1,0:T(8,128)(2,1)}, u32[]{:S(2)}) copy-start(bf16[8,8192]{1,0:T(8,128)(2,1)} %shard_map.103) | copy-start | bytes 393220
  25.6 30.7 %collective-permute-start.2 = (bf16[1024,512]{1,0:T(8,128)(2,1)S(1)}, bf16[1024,512]{1,0:T(8,128)(2,1)}, u32[]{:S(2)}, u32[]{:S(2)}) collective-permute-start(bf16[1024,512]{1,0:T(8,128)(2,1)S(1)} %fusion.mine), channel_id=1, source_target_pairs={{0,1},{1,0},{2,3},{3,2},{4,5},{5,4},{6,7},{7,6},{8,9},{9,8},{10,11... | collective-permute-start | bytes 3145736 | tf_op jit(solution)/shard_map/ppermute | solution.py:187
  58.8 0.8 copy-start
  59.6 15.9 %copy-start.2 = (f32[8,8192]{1,0:T(8,128)S(1)}, f32[8,8192]{1,0:T(8,128)}, u32[]{:S(2)}) copy-start(f32[8,8192]{1,0:T(8,128)} %convert_reduce_fusion) | copy-start | bytes 786436
  59.6 20.1 %all-to-all-start.1 = ((bf16[4,128,512]{2,1,0:T(8,128)(2,1)}), bf16[4,128,512]{2,1,0:T(8,128)(2,1)S(1)}, u32[]{:S(2)}, u32[]{:S(2)}) async-start(bf16[4,128,512]{2,1,0:T(8,128)(2,1)} %copy-done), calls=%async_computation.1 | async-start | bytes 1048576 | tf_op jit(solution)/shard_map/all_to_all | solution.py:20
  69.5 33.6 %copy-start.4 = (bf16[1,8,8192]{2,1,0:T(8,128)(2,1)S(1)}, bf16[1,8,8192]{2,1,0:T(8,128)(2,1)}, u32[]{:S(2)}) copy-start(bf16[1,8,8192]{2,1,0:T(8,128)(2,1)} %param.13) | copy-start | bytes 393220
  70.5 35.2 %collective-permute-start.1 = (bf16[512,1024]{1,0:T(8,128)(2,1)}, bf16[512,1024]{1,0:T(8,128)(2,1)}, u32[]{:S(2)}, u32[]{:S(2)}) collective-permute-start(bf16[512,1024]{1,0:T(8,128)(2,1)} %constant_dynamic-slice_fusion), channel_id=1, source_target_pairs={{0,1},{1,0},{2,3},{3,2},{4,5},{5,4},{6,7},{7,6},{8,9},{9,8},{10,11... | collective-permute-start | bytes 3145736 | tf_op jit(solution)/shard_map/ppermute | solution.py:202
  76.2 26.8 %collective-permute-start.4 = (bf16[8,8192]{1,0:T(8,128)(2,1)}, bf16[8,8192]{1,0:T(8,128)(2,1)}, u32[]{:S(2)}, u32[]{:S(2)}) collective-permute-start(bf16[8,8192]{1,0:T(8,128)(2,1)} %convert_element_type.92), channel_id=1, source_target_pairs={{0,64},{8,72},{16,80},{24,88},{32,96},{40,104},{48,112},{56,120},{... | collective-permute-start | bytes 393224 | tf_op jit(solution)/shard_map/ppermute | solution.py:165
  95.7 10.1 %collective-permute-start.3 = (bf16[512,512]{1,0:T(8,128)(2,1)S(1)}, bf16[512,512]{1,0:T(8,128)(2,1)S(1)}, u32[]{:S(2)}, u32[]{:S(2)}) collective-permute-start(bf16[512,512]{1,0:T(8,128)(2,1)S(1)} %bitcast.39), channel_id=1, source_target_pairs={{0,1},{1,0},{2,3},{3,2},{4,5},{5,4},{6,7},{7,6},{8,9},{9,8},{10,11... | collective-permute-start | bytes 1572872 | tf_op jit(solution)/shard_map/ppermute | solution.py:213
